TPU v7x, 128 devices: a whole 4x4x4 slice. The times are simulated.
128 devices in a mesh: row: 8 (over x_lo, z), col: 16 (over x_hi, y, core).
Axes of the slice: x: 4 (x_hi: 2, x_lo: 2; x = x_hi * 2 + x_lo), y: 4, z: 4, core: 2. Of those that a mesh axis runs over, the one named last changes fastest.
Arguments:
- object_field: float32 [2, 8192, 16384], P(None, 'row', 'col'), may hold values from -6 to 6
- illumination: float32 [2, 128, 128], replicated, may hold values from -6 to 6
- positions: int32 [8, 16, 64, 2], P('row', 'col'), may hold values from 0 to 1023
- slot_counts: int32 [8, 16], P('row', 'col'), may hold values from 16 to 64, as said below
- amplitudes: float32 [8, 16, 64, 128, 128], P('row', 'col'), may hold values from 0.3 to 3
Outputs:
- object_new: float32 [2, 8192, 16384], P(None, 'row', 'col')
- probe_new: float32 [2, 128, 128], replicated
Inputs may be any that keep to these rules, and one draw needn't show every extreme that they name: `slot_counts`: devices at the border of the mesh use at most 32 slots; some inner device uses all 64.
All inputs are finite; a program needn't handle non-finite values.
Results may differ from a plain program's by a relative error of at most 0.0003.
Values sent between devices are 32-bit elements; how exact they have to be, the bound alone decides.
A program may use at most 128 MiB of HBM per device.

v0:
```python
import math

import jax
import jax.numpy as jnp
from jax import lax
from jax.sharding import PartitionSpec as P

floor_value = 0.5
step_object = 0.25


def extended_2(cells, sides, width):
    for axis, dim in sides:
        count = lax.axis_size(axis)
        ends = count - 1
        head = lax.slice_in_dim(cells, 0, width, axis=dim)
        tail = lax.slice_in_dim(cells, cells.shape[dim] - width, cells.shape[dim], axis=dim)
        cells = jnp.concatenate(
            [
                lax.ppermute(tail, axis, [(i, (i + 1) % count) for i in range(ends)]),
                cells,
                lax.ppermute(head, axis, [((i + 1) % count, i) for i in range(ends)]),
            ],
            axis=dim,
        )
    return cells


def left_apply(matrix, stack):
    return jnp.einsum("kn,snm->skm", matrix, stack, precision=lax.Precision.HIGHEST)


def right_apply(stack, matrix):
    return jnp.einsum("skn,nm->skm", stack, matrix, precision=lax.Precision.HIGHEST)


def fold_edges(extended, axis_dim, half_width):
    length = extended.shape[axis_dim]
    middle = lax.slice_in_dim(extended, 2 * half_width, length - 2 * half_width, axis=axis_dim)
    inner_len = middle.shape[axis_dim]
    lower_band = lax.slice_in_dim(extended, 0, half_width, axis=axis_dim)
    upper_band = lax.slice_in_dim(extended, length - half_width, length, axis=axis_dim)
    widths_low = [(0, 0), (0, 0), (0, 0)]
    widths_up = [(0, 0), (0, 0), (0, 0)]
    widths_low[axis_dim] = (0, inner_len - half_width)
    widths_up[axis_dim] = (inner_len - half_width, 0)
    return middle + jnp.pad(lower_band, widths_low) + jnp.pad(upper_band, widths_up)


def shards(object_field, illumination, positions, slot_counts, amplitudes):
    patch_len = illumination.shape[-1]
    half_width = patch_len // 2
    capacity = positions.shape[2]
    padded = extended_2(object_field, (("row", 1), ("col", 2)), half_width)
    zero_index = jnp.int32(0)
    freq_ids = jnp.arange(patch_len, dtype=jnp.int32)
    phase_ids = freq_ids[:, None] * freq_ids[None, :] % patch_len
    angles = phase_ids.astype(jnp.float32) * (2.0 * math.pi / patch_len)
    cosine = jnp.cos(angles) / math.sqrt(patch_len)
    sine_table = jnp.sin(angles) / math.sqrt(patch_len)
    probe_real = illumination[0]
    probe_imag = illumination[1]
    offsets = positions[0, 0]
    count_here = slot_counts[0, 0]
    amp_here = amplitudes[0, 0]
    row_starts = offsets[:, 0]
    col_starts = offsets[:, 1]

    def extract(starts):
        return lax.dynamic_slice(
            padded, (zero_index, starts[0], starts[1]), (2, patch_len, patch_len)
        )

    patches = lax.map(extract, (row_starts, col_starts))
    obj_real = patches[:, 0]
    obj_imag = patches[:, 1]
    wave_real = probe_real * obj_real - probe_imag * obj_imag
    wave_imag = probe_real * obj_imag + probe_imag * obj_real
    half_real = left_apply(cosine, wave_real) + left_apply(sine_table, wave_imag)
    half_imag = left_apply(cosine, wave_imag) - left_apply(sine_table, wave_real)
    spec_real = right_apply(half_real, cosine) + right_apply(half_imag, sine_table)
    spec_imag = right_apply(half_imag, cosine) - right_apply(half_real, sine_table)
    modulus = jnp.sqrt(spec_real * spec_real + spec_imag * spec_imag)
    factor = amp_here / jnp.maximum(modulus, floor_value)
    proj_real = factor * spec_real
    proj_imag = factor * spec_imag
    back_real = left_apply(cosine, proj_real) - left_apply(sine_table, proj_imag)
    back_imag = left_apply(cosine, proj_imag) + left_apply(sine_table, proj_real)
    new_real = right_apply(back_real, cosine) - right_apply(back_imag, sine_table)
    new_imag = right_apply(back_imag, cosine) + right_apply(back_real, sine_table)
    live = (jnp.arange(capacity, dtype=jnp.int32) < count_here).astype(jnp.float32)[:, None, None]
    change_real = (new_real - wave_real) * live
    change_imag = (new_imag - wave_imag) * live
    term_real = probe_real * change_real + probe_imag * change_imag
    term_imag = probe_real * change_imag - probe_imag * change_real
    probe_real_grad = jnp.sum(obj_real * change_real + obj_imag * change_imag, axis=0)
    probe_imag_grad = jnp.sum(obj_real * change_imag - obj_imag * change_real, axis=0)
    terms = jnp.stack([term_real, term_imag], axis=1)

    def add_slot(slot, grad_now):
        where = (zero_index, row_starts[slot], col_starts[slot])
        window = lax.dynamic_slice(grad_now, where, (2, patch_len, patch_len))
        return lax.dynamic_update_slice(grad_now, window + terms[slot], where)

    gradient = lax.fori_loop(0, capacity, add_slot, jnp.zeros_like(padded))
    probe_total = lax.psum(jnp.stack([probe_real_grad, probe_imag_grad]), ("row", "col"))
    rate = (capacity * lax.axis_size("row") * lax.axis_size("col")) ** (-0.5)
    probe_new = illumination + rate * probe_total
    extended = extended_2(gradient, (("row", 1), ("col", 2)), half_width)
    returned = fold_edges(fold_edges(extended, 1, half_width), 2, half_width)
    object_new = object_field + step_object * returned
    return (object_new, probe_new)


def solution(mesh):
    placed = (
        P(None, "row", "col"),
        P(),
        P("row", "col", None, None),
        P("row", "col"),
        P("row", "col", None, None, None),
    )
    return jax.shard_map(
        shards, mesh=mesh, in_specs=placed, out_specs=(P(None, "row", "col"), P()), check_vma=False
    )
```

profile of v0, /device:TPU:6, one launch (start us, length us, event | category | flops | bytes accessed | tf_op | source)
XLA Modules:
  0.0 1526.6 jit_solution(14320489926537511766)
XLA Ops:
  16.6 8.7 copy.80
  28.2 11.4 concatenate.12
  42.8 7.3 collective-permute-start.3
  57.5 8.6 pad_maximum_fusion.1
  66.1 443.1 %while.23 = (s32[]{:T(128)}, f32[64,2,128,128]{3,2,0,1:T(8,128)}, s32[64]{0:T(128)S(1)}, s32[64]{0:T(128)S(1)}, f32[2,1152,1152]{1,2,0:T(8,128)}, /*index=5*/s32[]{:T(128)}, s32[]{:T(128)}, s32[]{:T(128)}) while((s32[]{:T(128)}, f32[64,2,128,128]{3,2,0,1:T(8,128)}, s32[64]{0:T(128)S(1)}, s32[64]{0:T(128)S(1)}, f32[2,1152,1152]{1,2,0:T(8,128)}, ...), condition=%wide.region_1.2_spmd, body=%wide.region_0.1_spmd.sunk | while | flops 8 | bytes 787129 | solution.py:74
  521.0 7.6 fusion.58
  528.6 7.2 convolution_subtract_fusion.1
  542.8 7.3 fusion.14
  557.2 7.3 fusion.30
  564.6 7.2 fusion.33
  571.8 10.6 fusion.55
  582.3 8.6 fusion.52
  591.0 9.3 convolution_add_fusion
  607.3 8.7 fusion.8
  616.0 12.1 convolution_subtract_fusion
  628.1 10.0 subtract_multiply_fusion
  638.1 14.3 fusion.25
  663.5 633.2 %while.24 = (s32[]{:T(128)}, f32[2,1152,1152]{2,1,0:T(8,128)}, s32[64]{0:T(128)S(1)}, s32[64]{0:T(128)S(1)}, f32[64,2,128,128]{3,2,0,1:T(8,128)}, /*index=5*/s32[]{:T(128)}, s32[]{:T(128)}, s32[]{:T(128)}) while((s32[]{:T(128)}, f32[2,1152,1152]{2,1,0:T(8,128)}, s32[64]{0:T(128)S(1)}, s32[64]{0:T(128)S(1)}, f32[64,2,128,128]{3,2,0,1:T(8,128)}, ...), condition=%wide.region_3.4_spmd, body=%wide.region_2.3_spmd.sunk | while | flops 32776 | bytes 655553 | solution.py:105
  1307.1 12.9 copy.78
  1320.8 13.9 concatenate.14
  1338.0 7.3 collective-permute-start.7
  1346.0 136.6 %all-reduce.4.cloned.1.call-done = f32[2,128,128]{2,1,0:T(8,128)} async-done(((f32[2,128,128]{2,1,0:T(8,128)}), f32[2,128,128]{2,1,0:T(8,128)}) %all-reduce.4.cloned.1.call-update) | async-done | bytes 131088 | tf_op jit(solution)/shard_map/psum | solution.py:106
  1497.8 13.1 fusion.5
  1510.9 8.7 copy.81
  (652 shorter events, 677.2 us)
Async XLA Ops:
  7.2 1475.4 %all-reduce.4.cloned.1.call-start = ((), (), s32[]{:S(2)}) async-start(), calls=%async_computation | async-start | bytes 262144 | tf_op jit(solution)/shard_map/psum | solution.py:106
  8.5 18.1 %collective-permute-start = (f32[2,64,1024]{2,1,0:T(8,128)S(1)}, f32[2,64,1024]{2,1,0:T(8,128)S(1)}, u32[]{:S(2)}, u32[]{:S(2)}) collective-permute-start(f32[2,64,1024]{2,1,0:T(8,128)S(1)} %get-tuple-element.189), channel_id=1, source_target_pairs={{0,16},{16,32},{32,48},{48,64},{64,80},{80,96},{96,112},{1,17},{17... | collective-permute-start | bytes 1572872 | tf_op jit(solution)/shard_map/ppermute | solution.py:20
  12.3 15.5 %collective-permute-start.1 = (f32[2,64,1024]{2,1,0:T(8,128)S(1)}, f32[2,64,1024]{2,1,0:T(8,128)S(1)}, u32[]{:S(2)}, u32[]{:S(2)}) collective-permute-start(f32[2,64,1024]{2,1,0:T(8,128)S(1)} %get-tuple-element.188), channel_id=1, source_target_pairs={{16,0},{32,16},{48,32},{64,48},{80,64},{96,80},{112,96},{17,1},{33... | collective-permute-start | bytes 1572872 | tf_op jit(solution)/shard_map/ppermute | solution.py:22
  28.1 22.6 %copy-start.10 = (s32[1,1,64,2]{2,3,1,0:T(2,128)S(1)}, s32[1,1,64,2]{2,3,1,0:T(2,128)}, u32[]{:S(2)}) copy-start(s32[1,1,64,2]{2,3,1,0:T(2,128)} %param.11) | copy-start | bytes 1540
  28.1 22.6 %copy-start.5 = (f32[2,128,128]{2,1,0:T(8,128)S(1)}, f32[2,128,128]{2,1,0:T(8,128)}, u32[]{:S(2)}) copy-start(f32[2,128,128]{2,1,0:T(8,128)} %param.10) | copy-start | bytes 393220
  40.9 14.8 collective-permute-start.2
  42.8 14.6 collective-permute-start.3
  50.8 458.4 %copy-start.3 = (f32[128,128]{1,0:T(8,128)}, f32[128,128]{1,0:T(8,128)S(1)}, u32[]{:S(2)}) copy-start(f32[128,128]{1,0:T(8,128)S(1)} %get-tuple-element.190) | copy-start | bytes 196612
  50.8 458.4 %copy-start.4 = (f32[128,128]{1,0:T(8,128)}, f32[128,128]{1,0:T(8,128)S(1)}, u32[]{:S(2)}) copy-start(f32[128,128]{1,0:T(8,128)S(1)} %get-tuple-element.191) | copy-start | bytes 196612
  564.5 26.4 %copy-start = (f32[64,128,128]{2,1,0:T(8,128)}, f32[64,128,128]{2,1,0:T(8,128)S(1)}, u32[]{:S(2)}) copy-start(f32[64,128,128]{2,1,0:T(8,128)S(1)} %fusion.30) | copy-start | bytes 12582916
  564.6 7.2 copy-start.11
  571.8 19.2 %copy-start.2 = (f32[64,128,128]{2,1,0:T(8,128)}, f32[64,128,128]{2,1,0:T(8,128)S(1)}, u32[]{:S(2)}) copy-start(f32[64,128,128]{2,1,0:T(8,128)S(1)} %fusion.33) | copy-start | bytes 12582916
  607.3 8.7 copy-start.1
  607.3 30.8 %slice-start.3 = ((s8[8388608]{0:T(1024)(128)(4,1)}), s8[4194304]{0:T(1024)(128)(4,1)S(1)}, s32[]{:S(2)}) async-start(s8[8388608]{0:T(1024)(128)(4,1)} %bitcast.153), calls=%async_computation.4 | async-start | bytes 8388608
  616.0 22.1 %slice-start.4 = ((s8[8388608]{0:T(1024)(128)(4,1)}), s8[4194304]{0:T(1024)(128)(4,1)S(1)}, s32[]{:S(2)}) async-start(s8[8388608]{0:T(1024)(128)(4,1)} %bitcast.153), calls=%async_computation.5 | async-start | bytes 8388608
  1298.0 22.0 %collective-permute-start.4 = (f32[2,64,1152]{2,1,0:T(8,128)S(1)}, f32[2,64,1152]{2,1,0:T(8,128)S(1)}, u32[]{:S(2)}, u32[]{:S(2)}) collective-permute-start(f32[2,64,1152]{2,1,0:T(8,128)S(1)} %get-tuple-element.179), channel_id=1, source_target_pairs={{0,16},{16,32},{32,48},{48,64},{64,80},{80,96},{96,112},{1,17},{17... | collective-permute-start | bytes 1769480 | tf_op jit(solution)/shard_map/ppermute | solution.py:20
  1301.3 19.1 %collective-permute-start.5 = (f32[2,64,1152]{2,1,0:T(8,128)S(1)}, f32[2,64,1152]{2,1,0:T(8,128)S(1)}, u32[]{:S(2)}, u32[]{:S(2)}) collective-permute-start(f32[2,64,1152]{2,1,0:T(8,128)S(1)} %get-tuple-element.178), channel_id=1, source_target_pairs={{16,0},{32,16},{48,32},{64,48},{80,64},{96,80},{112,96},{17,1},{33... | collective-permute-start | bytes 1769480 | tf_op jit(solution)/shard_map/ppermute | solution.py:22
  1320.7 24.6 %copy-start.7 = (f32[128,128]{1,0:T(8,128)S(1)}, f32[128,128]{1,0:T(8,128)}, u32[]{:S(2)}) copy-start(f32[128,128]{1,0:T(8,128)} %get-tuple-element.154) | copy-start | bytes 196612
  1320.8 24.6 %copy-start.8 = (f32[128,128]{1,0:T(8,128)S(1)}, f32[128,128]{1,0:T(8,128)}, u32[]{:S(2)}) copy-start(f32[128,128]{1,0:T(8,128)} %get-tuple-element.155) | copy-start | bytes 196612
  1320.8 161.8 %copy-start.6 = (f32[2,128,128]{2,1,0:T(8,128)S(1)}, f32[2,128,128]{2,1,0:T(8,128)}, u32[]{:S(2)}) copy-start(f32[2,128,128]{2,1,0:T(8,128)} %param.10) | copy-start | bytes 393220
  1336.1 148.2 %collective-permute-start.6 = (f32[2,1280,64]{1,2,0:T(8,128)S(1)}, f32[2,1280,64]{1,2,0:T(8,128)S(1)}, u32[]{:S(2)}, u32[]{:S(2)}) collective-permute-start(f32[2,1280,64]{1,2,0:T(8,128)S(1)} %get-tuple-element.176), channel_id=1, source_target_pairs={{0,1},{1,2},{2,3},{3,4},{4,5},{5,6},{6,7},{7,8},{8,9},{9,10},{10,1... | collective-permute-start | bytes 1966088 | tf_op jit(solution)/shard_map/ppermute | solution.py:20
  1338.0 146.3 %collective-permute-start.7 = (f32[2,1280,64]{1,2,0:T(8,128)S(1)}, f32[2,1280,64]{1,2,0:T(8,128)S(1)}, u32[]{:S(2)}, u32[]{:S(2)}) collective-permute-start(f32[2,1280,64]{1,2,0:T(8,128)S(1)} %get-tuple-element.177), channel_id=1, source_target_pairs={{1,0},{2,1},{3,2},{4,3},{5,4},{6,5},{7,6},{8,7},{9,8},{10,9},{11,1... | collective-permute-start | bytes 1966088 | tf_op jit(solution)/shard_map/ppermute | solution.py:22
  1482.6 8.6 slice-start
  1484.3 6.9 copy-start.9
  (2 other events, 13.9 us)
Sparse Core Ops, SparseCore 0:
  1346.1 136.4 all-reduce.3
where the time goes:
time: 1550 us; the launch traced here: 1530 us
  local copies, waits for them, and re-layouts  575 us (37%)
  loops' own time  496 us (32%)
  waiting for transfers between devices  145 us (9%)
  matrix products  138 us (9%)
  other arithmetic  121 us (8%)
  starting transfers between devices  35.6 us (2%)
    another operation x1, loops' own time, shards(): gradient = lax.fori_loop(0, capacity, add_slot, jnp.zeros_like(padded))  249 us
    another operation x1, loops' own time, shards(): patches = lax.map(extract, (row_starts, col_starts))  247 us
    dynamic_update_slice x64, local copies, waits for them, and re-layouts, add_slot(): return lax.dynamic_update_slice(grad_now, window + terms[slot], where)  235 us
    psum x1, waiting for transfers between devices, shards(): lax.psum(jnp.stack([probe_real_grad, probe_imag_grad]), ('row', 'col'))  137 us
    dynamic_slice x128, local copies, waits for them, and re-layouts, shards(): patches = lax.map(extract, (row_starts, col_starts))  78.6 us
    dynamic_slice x128, local copies, waits for them, and re-layouts, extract(): lax.dynamic_slice(padded, (zero_index, starts[0], starts[1]), (2, patch_l...  75.1 us
    dynamic_slice x128, local copies, waits for them, and re-layouts, add_slot(): where = (zero_index, row_starts[slot], col_starts[slot])  74.9 us
    add x64, other arithmetic, add_slot(): return lax.dynamic_update_slice(grad_now, window + terms[slot], where)  73.6 us
  transfers between devices with their start and end apart: 9, of which 5 were waited for; matrix products, arithmetic and copies ran while one was open for 2% of the time, Pallas kernels for 0%

commit v1 on v0

v1 whole, which is shorter than its diff:
```python
import functools
import math

import jax
import jax.numpy as jnp
import ml_dtypes
import numpy as np
from jax import lax
from jax.experimental import pallas as pl
from jax.experimental.pallas import tpu as pltpu
from jax.sharding import PartitionSpec as P

MESH = pl.DeviceIdType.MESH
PATCH = 128
HALF = 64
TILE = 1024
CAP = 64
LANE_TILES = TILE // PATCH
GROUP = 8
step_object = 0.25
DIRS = ((1, 0), (-1, 0), (0, 1), (0, -1), (1, 1), (1, -1), (-1, 1), (-1, -1))
SMALL_ROWS = 16
ANY = pl.BlockSpec(memory_space=pl.ANY)
IN_VMEM = pl.BlockSpec(memory_space=pltpu.VMEM)
IN_SMEM = pl.BlockSpec(memory_space=pltpu.SMEM)


def f32(*shape):
    return jax.ShapeDtypeStruct(shape, jnp.float32)


STRIPS = (
    f32(2, HALF, TILE), f32(2, HALF, TILE), f32(2, TILE, PATCH), f32(2, TILE, PATCH),
    f32(2, HALF, PATCH), f32(2, HALF, PATCH), f32(2, HALF, PATCH), f32(2, HALF, PATCH),
)


def tables():
    ids = np.arange(PATCH)
    angles = (np.outer(ids, ids) % PATCH) * (2 * math.pi / PATCH)
    cosine, sine = np.cos(angles) / math.sqrt(PATCH), np.sin(angles) / math.sqrt(PATCH)
    forward = np.block([[cosine, -sine], [sine, cosine]])
    out = []
    for matrix in (forward, forward.T):
        high = matrix.astype(np.float32).astype(ml_dtypes.bfloat16)
        out += [high, (matrix - high.astype(np.float64)).astype(np.float32).astype(ml_dtypes.bfloat16)]
    return np.stack(out)


def place():
    return lax.axis_index("row"), lax.axis_index("col"), lax.axis_size("row"), lax.axis_size("col")


def exists(da, db):
    a, b, rows, cols = place()
    return (a + da >= 0) & (a + da < rows) & (b + db >= 0) & (b + db < cols)


def strip_copy(d, src, dst, send_sem, recv_sem):
    a, b, _, _ = place()
    da, db = DIRS[d]
    return pltpu.make_async_remote_copy(
        src_ref=src, dst_ref=dst, send_sem=send_sem.at[d], recv_sem=recv_sem.at[d],
        device_id=(a + da, b + db), device_id_type=MESH,
    )


def start_strips(srcs, dsts, send_sem, recv_sem):
    for d, (da, db) in enumerate(DIRS):
        @pl.when(exists(da, db))
        def _():
            strip_copy(d, srcs[d], dsts[d], send_sem, recv_sem).start()


def wait_strips(srcs, dsts, send_sem, recv_sem):
    for d, (da, db) in enumerate(DIRS):
        @pl.when(exists(-da, -db))
        def _():
            strip_copy(d, srcs[d], dsts[d], send_sem, recv_sem).wait_recv()

        @pl.when(exists(da, db))
        def _():
            strip_copy(d, srcs[d], dsts[d], send_sem, recv_sem).wait_send()


def greet_strips(barrier, dirs):
    a, b, _, _ = place()
    for da, db in dirs:
        @pl.when(exists(da, db))
        def _():
            pl.semaphore_signal(barrier, inc=1, device_id=(a + da, b + db), device_id_type=MESH)


def halo_kernel(obj, *refs):
    strips, (send_sem, recv_sem) = refs[:8], refs[8:]
    a, b, rows, cols = place()
    barrier = pltpu.get_barrier_semaphore()
    greet_strips(barrier, DIRS)
    high = 1 + (a > 0).astype(jnp.int32) + (a < rows - 1).astype(jnp.int32)
    wide = 1 + (b > 0).astype(jnp.int32) + (b < cols - 1).astype(jnp.int32)
    pl.semaphore_wait(barrier, high * wide - 1)
    row_part = {1: slice(TILE - HALF, TILE), -1: slice(0, HALF), 0: slice(0, TILE)}
    col_part = {1: slice(TILE - PATCH, TILE), -1: slice(0, PATCH), 0: slice(0, TILE)}
    srcs = [obj.at[:, row_part[da], col_part[db]] for da, db in DIRS]
    start_strips(srcs, strips, send_sem, recv_sem)
    wait_strips(srcs, strips, send_sem, recv_sem)


def exchange_object(obj):
    return pl.pallas_call(
        halo_kernel,
        out_shape=STRIPS,
        in_specs=[ANY],
        out_specs=(ANY,) * 8,
        scratch_shapes=[pltpu.SemaphoreType.DMA((8,)), pltpu.SemaphoreType.DMA((8,))],
        compiler_params=pltpu.CompilerParams(collective_id=0, has_side_effects=True),
    )(obj)


def split(x):
    high = x.astype(jnp.bfloat16)
    return high, (x - high.astype(jnp.float32)).astype(jnp.bfloat16)


def dot(x, y):
    return jnp.dot(x, y, preferred_element_type=jnp.float32)


def right(x, high, low):
    xh, xl = split(x)
    return dot(xh, high) + dot(xl, high) + dot(xh, low)


def left(high, low, x):
    xh, xl = split(x)
    return dot(high, xh) + dot(high, xl) + dot(low, xh)


def border(d):
    da, db = DIRS[d]
    rows = {1: slice(0, HALF), -1: slice(HALF + TILE, 2 * HALF + TILE), 0: slice(HALF, HALF + TILE)}[da]
    return rows, {1: 0, -1: LANE_TILES + 1, 0: None}[db]


def border_views(buf, strip, d):
    rows, tile = border(d)
    if tile is not None:
        return [(strip, buf.at[:, tile, rows, :])]
    return [
        (strip.at[p, :, t * PATCH:(t + 1) * PATCH], buf.at[p, t + 1, rows, :])
        for p in range(2) for t in range(LANE_TILES)
    ]


def slots_kernel(pos, cnt, obj, ill, amp, tab, *refs):
    halo, out, edges, hout = refs[:8], refs[8], refs[9:17], refs[17]
    ob, gr, hacc, ampbuf, sem, asem, osem = refs[18:]
    count = cnt[0, 0]
    steps = (count + GROUP - 1) // GROUP
    body_copies = [
        pltpu.make_async_copy(obj.at[p, :, t * PATCH:(t + 1) * PATCH], ob.at[p, t + 1, HALF:HALF + TILE, :], sem.at[p * 8 + t])
        for p in range(2) for t in range(LANE_TILES)
    ]
    for copy in body_copies:
        copy.start()

    def amp_copy(i):
        return pltpu.make_async_copy(amp.at[0, 0, pl.ds(i * GROUP, GROUP)], ampbuf.at[i], asem.at[i])

    @pl.loop(0, steps)
    def _(i):
        amp_copy(i).start()

    halo_copies = []
    for d in range(8):
        views = border_views(ob, halo[d], d)
        halo_copies.append([pltpu.make_async_copy(src, dst, osem.at[d, n]) for n, (src, dst) in enumerate(views)])
    for d, (da, db) in enumerate(DIRS):
        @pl.when(exists(-da, -db))
        def _():
            for copy in halo_copies[d]:
                copy.start()

        @pl.when(jnp.logical_not(exists(-da, -db)))
        def _():
            rows, tile = border(d)
            for p in range(2):
                for t in range(1, LANE_TILES + 1) if tile is None else (tile,):
                    ob[p, t, rows, :] = jnp.zeros((rows.stop - rows.start, PATCH), jnp.float32)

    zero = jnp.zeros((PATCH, PATCH), jnp.float32)

    @pl.loop(0, (TILE + PATCH) // PATCH)
    def _(i):
        rows = pl.ds(pl.multiple_of(i * PATCH, PATCH), PATCH)
        for p in range(2):
            for t in range(LANE_TILES + 2):
                gr[p, t, rows, :] = zero
            ob[p, LANE_TILES + 2, rows, :] = zero
    hacc[...] = jnp.zeros_like(hacc)
    for copy in body_copies:
        copy.wait()
    for d, (da, db) in enumerate(DIRS):
        @pl.when(exists(-da, -db))
        def _():
            for copy in halo_copies[d]:
                copy.wait()
    lane = lax.broadcasted_iota(jnp.int32, (PATCH, PATCH), 1)

    def step(i, carry):
        amp_copy(i).wait()
        fh, fl, bh, bl = tab[0], tab[1], tab[2], tab[3]
        info, news = [], []
        for g in range(GROUP):
            s = i * GROUP + g
            live = s < count
            rows = pl.ds(pos[0, 0, s, 0], PATCH)
            column = pos[0, 0, s, 1] + HALF
            t, shift = column >> 7, column & (PATCH - 1)
            first = lane >= shift
            ta, tb = jnp.where(live, t, LANE_TILES + 2), jnp.where(live, t + 1, LANE_TILES + 2)
            o_r = jnp.where(first, ob[0, ta, rows, :], ob[0, tb, rows, :])
            o_i = jnp.where(first, ob[1, ta, rows, :], ob[1, tb, rows, :])
            p_r, p_i = pltpu.roll(ill[0], shift, 1), pltpu.roll(ill[1], shift, 1)
            info.append((rows, t, shift, first, o_r, o_i, p_r, p_i, p_r * o_r - p_i * o_i, p_r * o_i + p_i * o_r))
        for g in range(0, GROUP, 2):
            x = jnp.concatenate([jnp.concatenate(info[k][8:10], 1) for k in (g, g + 1)], 0)
            y = right(x, fh, fl)
            y = jnp.concatenate([jnp.concatenate([y[:PATCH, c:c + PATCH], y[PATCH:, c:c + PATCH]], 1) for c in (0, PATCH)], 0)
            z = left(bh, bl, y)
            z_r, z_i = z[:PATCH], z[PATCH:]
            a = jnp.concatenate([ampbuf[i, g], ampbuf[i, g + 1]], 1)
            factor = a * jnp.minimum(lax.rsqrt(z_r * z_r + z_i * z_i), 2.0)
            r = left(fh, fl, jnp.concatenate([factor * z_r, factor * z_i], 0))
            r = jnp.concatenate([jnp.concatenate([r[:PATCH, c:c + PATCH], r[PATCH:, c:c + PATCH]], 1) for c in (0, PATCH)], 0)
            n = right(r, bh, bl)
            news += [(n[:PATCH, :PATCH], n[:PATCH, PATCH:]), (n[PATCH:, :PATCH], n[PATCH:, PATCH:])]
        for g in range(GROUP):
            rows, t, shift, first, o_r, o_i, p_r, p_i, w_r, w_i = info[g]
            c_r, c_i = news[g][0] - w_r, news[g][1] - w_i
            for p, term in ((0, p_r * c_r + p_i * c_i), (1, p_r * c_i - p_i * c_r)):
                now = jnp.where(first, gr[p, t, rows, :], gr[p, t + 1, rows, :]) + term
                pltpu.store(gr.at[p, t, rows, :], now, mask=first)
                pltpu.store(gr.at[p, t + 1, rows, :], now, mask=jnp.logical_not(first))
            back = PATCH - shift
            hacc[0:PATCH] += pltpu.roll(o_r * c_r + o_i * c_i, back, 1)
            hacc[PATCH:] += pltpu.roll(o_r * c_i - o_i * c_r, back, 1)
        return carry

    lax.fori_loop(0, steps, step, 0)
    hout[...] = hacc[...]
    last = []
    for d in range(8):
        da, db = DIRS[d]
        views = border_views(gr, edges[d], DIRS.index((-da, -db)))
        last += [pltpu.make_async_copy(dst, src, osem.at[d, n]) for n, (src, dst) in enumerate(views)]
    for copy in last:
        copy.start()
    for p in range(2):
        for t in range(LANE_TILES):
            @pl.loop(0, TILE // PATCH)
            def _(i):
                rows = pl.ds(pl.multiple_of(HALF + i * PATCH, HALF), PATCH)
                ob[p, t + 1, rows, :] += step_object * gr[p, t + 1, rows, :]
            copy = pltpu.make_async_copy(
                ob.at[p, t + 1, HALF:HALF + TILE, :], out.at[p, :, t * PATCH:(t + 1) * PATCH], sem.at[p * 8 + t])
            copy.start()
            last.append(copy)
    for copy in last:
        copy.wait()


def run_slots(positions, slot_counts, obj, ill, amplitudes, halo):
    return pl.pallas_call(
        slots_kernel,
        out_shape=(f32(2, TILE, TILE),) + STRIPS + (f32(2 * PATCH, PATCH),),
        in_specs=[IN_SMEM, IN_SMEM, ANY, IN_VMEM, ANY, IN_VMEM] + [ANY] * 8,
        out_specs=(ANY,) * 9 + (IN_VMEM,),
        scratch_shapes=[
            pltpu.VMEM((2, LANE_TILES + 3, TILE + PATCH, PATCH), jnp.float32),
            pltpu.VMEM((2, LANE_TILES + 2, TILE + PATCH, PATCH), jnp.float32),
            pltpu.VMEM((2 * PATCH, PATCH), jnp.float32),
            pltpu.VMEM((CAP // GROUP, GROUP, PATCH, PATCH), jnp.float32),
            pltpu.SemaphoreType.DMA((16,)), pltpu.SemaphoreType.DMA((CAP // GROUP,)), pltpu.SemaphoreType.DMA((8, 16)),
        ],
        compiler_params=pltpu.CompilerParams(vmem_limit_bytes=50 * 2**20),
    )(positions, slot_counts, obj, ill, amplitudes, jnp.asarray(tables()), *halo)


def return_kernel(h, *refs):
    edges, strips, total = refs[:8], refs[8:16], refs[16]
    pieces, sums, gathered, send_sem, recv_sem, s1, r1, s2, r2, s3, r3 = refs[17:]
    a, b, rows, cols = place()
    barrier = pltpu.get_barrier_semaphore()
    greet_strips(barrier, DIRS[4:])

    def col_peer(k):
        return lax.rem(b + k, cols)

    def row_peer(k):
        return lax.rem(a + k, rows)

    @pl.loop(1, cols)
    def _(k):
        pl.semaphore_signal(barrier, inc=1, device_id=(a, col_peer(k)), device_id_type=MESH)

    @pl.loop(1, rows)
    def _(k):
        pl.semaphore_signal(barrier, inc=1, device_id=(row_peer(k), b), device_id_type=MESH)

    high = (a > 0).astype(jnp.int32) + (a < rows - 1).astype(jnp.int32)
    wide = (b > 0).astype(jnp.int32) + (b < cols - 1).astype(jnp.int32)
    pl.semaphore_wait(barrier, cols - 1 + rows - 1 + high * wide)

    def piece_rows(k):
        return pl.ds(pl.multiple_of(k * SMALL_ROWS, SMALL_ROWS), SMALL_ROWS)

    def scatter(peer, slot):
        return pltpu.make_async_remote_copy(
            src_ref=h.at[piece_rows(peer)], dst_ref=pieces.at[slot], send_sem=s1.at[peer], recv_sem=r1.at[slot],
            device_id=(a, peer), device_id_type=MESH)

    def share(peer, slot):
        return pltpu.make_async_remote_copy(
            src_ref=sums.at[slot], dst_ref=sums.at[slot], send_sem=s2.at[peer], recv_sem=r2.at[slot],
            device_id=(peer, b), device_id_type=MESH)

    def gather(peer, slot):
        return pltpu.make_async_remote_copy(
            src_ref=gathered.at[slot], dst_ref=gathered.at[slot], send_sem=s3.at[peer], recv_sem=r3.at[slot],
            device_id=(a, peer), device_id_type=MESH)

    @pl.loop(1, cols)
    def _(k):
        scatter(col_peer(k), b).start()

    start_strips(edges, strips, send_sem, recv_sem)
    pieces[b] = h[piece_rows(b), :]

    @pl.loop(1, cols)
    def _(k):
        scatter(b, col_peer(k)).wait_recv()

    sums[a] = jnp.sum(pieces[...], axis=0)

    @pl.loop(1, rows)
    def _(k):
        share(row_peer(k), a).start()

    @pl.loop(1, rows)
    def _(k):
        share(a, row_peer(k)).wait_recv()

    gathered[b] = jnp.sum(sums[...], axis=0)

    @pl.loop(1, cols)
    def _(k):
        gather(col_peer(k), b).start()

    @pl.loop(1, cols)
    def _(k):
        gather(b, col_peer(k)).wait_recv()

    total[...] = gathered[...]

    @pl.loop(1, cols)
    def _(k):
        scatter(col_peer(k), b).wait_send()
        gather(col_peer(k), b).wait_send()

    @pl.loop(1, rows)
    def _(k):
        share(row_peer(k), a).wait_send()

    wait_strips(edges, strips, send_sem, recv_sem)


def return_edges(h, edges):
    rows, cols = lax.axis_size("row"), lax.axis_size("col")
    dma = pltpu.SemaphoreType.DMA
    return pl.pallas_call(
        return_kernel,
        out_shape=STRIPS + (f32(cols, SMALL_ROWS, PATCH),),
        in_specs=[IN_VMEM] + [ANY] * 8,
        out_specs=(ANY,) * 8 + (IN_VMEM,),
        scratch_shapes=[
            pltpu.VMEM((cols, SMALL_ROWS, PATCH), jnp.float32), pltpu.VMEM((rows, SMALL_ROWS, PATCH), jnp.float32),
            pltpu.VMEM((cols, SMALL_ROWS, PATCH), jnp.float32), dma((8,)), dma((8,)),
            dma((cols,)), dma((cols,)), dma((rows,)), dma((rows,)), dma((cols,)), dma((cols,)),
        ],
        compiler_params=pltpu.CompilerParams(collective_id=1, has_side_effects=True),
    )(h, *edges)


def finish_kernel(rate, core, ill, total, *refs):
    strips, out, probe = refs[:8], refs[8], refs[9]
    top, bottom, west, east, sem = refs[10:]
    inner = slice(HALF, TILE - HALF)
    parts = (
        (top, out.at[:, 0:HALF, :]), (bottom, out.at[:, TILE - HALF:TILE, :]),
        (west, out.at[:, inner, 0:PATCH]), (east, out.at[:, inner, TILE - PATCH:TILE]),
    )
    reads = [pltpu.make_async_copy(hbm, vmem, sem.at[n]) for n, (vmem, hbm) in enumerate(parts)]
    writes = [pltpu.make_async_copy(vmem, hbm, sem.at[n]) for n, (vmem, hbm) in enumerate(parts)]
    for copy in reads:
        copy.start()
    probe[...] = ill[...] + rate * total[...]
    for copy in reads:
        copy.wait()
    lo, hi = slice(0, PATCH), slice(TILE - PATCH, TILE)
    adds = (
        ((top, slice(None), slice(None), slice(None)),),
        ((bottom, slice(None), slice(None), slice(None)),),
        ((west, slice(None), slice(None), inner), (top, slice(None), lo, slice(0, HALF)), (bottom, slice(None), lo, slice(TILE - HALF, TILE))),
        ((east, slice(None), slice(None), inner), (top, slice(None), hi, slice(0, HALF)), (bottom, slice(None), hi, slice(TILE - HALF, TILE))),
        ((top, slice(None), lo, slice(None)),), ((top, slice(None), hi, slice(None)),),
        ((bottom, slice(None), lo, slice(None)),), ((bottom, slice(None), hi, slice(None)),),
    )
    for d, (da, db) in enumerate(DIRS):
        @pl.when(exists(-da, -db))
        def _():
            for target, rows, cols, source in adds[d]:
                target[:, rows, cols] += step_object * strips[d][:, source, :]
    for copy in writes:
        copy.start()
    for copy in writes:
        copy.wait()


def finish(core, ill, total, strips):
    rate = (CAP * lax.axis_size("row") * lax.axis_size("col")) ** (-0.5)
    return pl.pallas_call(
        functools.partial(finish_kernel, rate),
        out_shape=(f32(2, TILE, TILE), f32(2, PATCH, PATCH)),
        in_specs=[ANY, IN_VMEM, IN_VMEM] + [IN_VMEM] * 8,
        out_specs=(ANY, IN_VMEM),
        input_output_aliases={0: 0},
        scratch_shapes=[
            pltpu.VMEM((2, HALF, TILE), jnp.float32), pltpu.VMEM((2, HALF, TILE), jnp.float32),
            pltpu.VMEM((2, TILE - PATCH, PATCH), jnp.float32), pltpu.VMEM((2, TILE - PATCH, PATCH), jnp.float32),
            pltpu.SemaphoreType.DMA((4,)),
        ],
        compiler_params=pltpu.CompilerParams(vmem_limit_bytes=32 * 2**20),
    )(core, ill, total.reshape(2, PATCH, PATCH), *strips)


def shards(object_field, illumination, positions, slot_counts, amplitudes):
    halo = exchange_object(object_field)
    core, *rest = run_slots(positions, slot_counts, object_field, illumination, amplitudes, halo)
    edges, h = rest[:8], rest[8]
    *strips, total = return_edges(h, edges)
    return finish(core, illumination, total, strips)


def solution(mesh):
    placed = (
        P(None, "row", "col"),
        P(),
        P("row", "col", None, None),
        P("row", "col"),
        P("row", "col", None, None, None),
    )
    return jax.shard_map(
        shards, mesh=mesh, in_specs=placed, out_specs=(P(None, "row", "col"), P()), check_vma=False
    )
```

time: 1550 us -> 146 us (0.09); the launches traced: 1530 us -> 143 us
  local copies, waits for them, and re-layouts: 575 us -> 19.7 us
  loops' own time: 496 us -> 0 us
  waiting for transfers between devices: 145 us -> 0 us
  matrix products: 138 us -> 0 us
  Pallas kernels: 0 us -> 122 us
  other arithmetic: 121 us -> 0 us
  starting transfers between devices: 35.6 us -> 0 us
    another operation x2 -> x0, loops' own time: 496 us -> none  [the longest x1 249 us: shards(): gradient = lax.fori_loop(0, capacity, add_slot, jnp.zeros_like(padded))]
    dynamic_update_slice x128 -> x0, local copies, waits for them, and re-layouts: 278 us -> none  [the longest x64 235 us: add_slot(): return lax.dynamic_update_slice(grad_now, window + terms[slot], where)]
    dynamic_slice x384 -> x0, local copies, waits for them, and re-layouts: 229 us -> none  [the longest x128 78.6 us: shards(): patches = lax.map(extract, (row_starts, col_starts))]
    dot_general x16 -> x0, matrix products: 138 us -> none  [the longest x8 69.6 us: left_apply(): jnp.einsum('kn,snm->skm', matrix, stack, precision=lax.Precision.HIGHEST)]
    psum x1 -> x0, waiting for transfers between devices: 137 us -> none  [shards(): lax.psum(jnp.stack([probe_real_grad, probe_imag_grad]), ('row', 'col'))]
    pallas_call x0 -> x4, Pallas kernels: none -> 122 us  [the longest x1 46.2 us: return_edges(): pl.pallas_call(return_kernel, out_shape=STRIPS + (f32(cols, SMALL_ROWS, P...]
    add x68 -> x0, other arithmetic: 98.5 us -> none  [the longest x64 73.6 us: add_slot(): return lax.dynamic_update_slice(grad_now, window + terms[slot], where)]
    ppermute x8 -> x0, starting transfers between devices: 35.6 us -> none  [the longest x4 24.6 us: extended_2(): lax.ppermute(head, axis, [((i + 1) % count, i) for i in range(ends)])]
  transfers between devices with their start and end apart: 9 -> 0, of which waited for: 5 -> 0; matrix products, arithmetic and copies ran while one was open for 2% -> 0% of each run, Pallas kernels for 0% -> 0%
where the time goes in v1:
time: 146 us; the launch traced here: 143 us
  Pallas kernels  122 us (84%)
  local copies, waits for them, and re-layouts  19.7 us (13%)
    pallas_call x1, Pallas kernels, return_edges(): pl.pallas_call(return_kernel, out_shape=STRIPS + (f32(cols, SMALL_ROWS, P...  46.2 us
    pallas_call x1, Pallas kernels, run_slots(): pl.pallas_call(slots_kernel, out_shape=(f32(2, TILE, TILE),) + STRIPS + (...  37.5 us
    pallas_call x1, Pallas kernels, exchange_object(): pl.pallas_call(halo_kernel, out_shape=STRIPS, in_specs=[ANY], out_specs=(...  33.9 us
    unnamed x49, local copies, waits for them, and re-layouts  19.7 us
    pallas_call x1, Pallas kernels, finish(): pl.pallas_call(functools.partial(finish_kernel, rate), out_shape=(f32(2,...  4.5 us

profile of v1, /device:TPU:6, one launch (start us, length us, event | category | flops | bytes accessed | tf_op | source)
XLA Modules:
  0.0 143.3 jit_solution(12123798077534593666)
XLA Ops:
  1.4 0.8 copy.9.pos
  2.1 33.9 %shard_map.77 = (f32[2,64,1024]{2,1,0:T(8,128)}, f32[2,64,1024]{2,1,0:T(8,128)}, f32[2,1024,128]{2,1,0:T(8,128)}, f32[2,1024,128]{2,1,0:T(8,128)}, f32[2,64,128]...) custom-call(f32[2,1024,1024]{2,1,0:T(8,128)} %obj.3), custom_call_target="tpu_custom_call" | custom-call | tf_op jit(solution)/shard_map/pallas_call | solution.py:110
  36.0 1.0 copy-done.6
  37.1 1.0 copy-done.7
  38.1 0.8 copy-done.16
  38.9 0.8 copy-done.17
  39.8 0.8 copy-done.18
  40.6 0.8 copy-done.19
  41.5 37.5 %shard_map.78 = (f32[2,1024,1024]{2,1,0:T(8,128)}, f32[2,64,1024]{2,1,0:T(8,128)S(1)}, f32[2,64,1024]{2,1,0:T(8,128)S(1)}, f32[2,1024,128]{2,1,0:T(8,128)}, f32[...) custom-call(s32[1,1,64,2]{3,2,1,0:T(8,128)S(1)} %copy.9.pos, ...), custom_call_target="tpu_custom_call" | custom-call | tf_op jit(solution)/shard_map/pallas_call | solution.py:274
  79.0 0.8 copy-done.3
  79.8 0.8 copy-done.4
  80.6 0.7 copy-done.11
  81.3 0.6 copy-done.12
  83.8 46.2 %shard_map.79 = (f32[2,64,1024]{2,1,0:T(8,128)}, f32[2,64,1024]{2,1,0:T(8,128)}, f32[2,1024,128]{2,1,0:T(8,128)}, f32[2,1024,128]{2,1,0:T(8,128)}, f32[2,64,128]...) custom-call(f32[256,128]{1,0:T(8,128)} %copy-done.11, ...), custom_call_target="tpu_custom_call" | custom-call | tf_op jit(solution)/shard_map/pallas_call | solution.py:381
  130.0 1.2 copy-done
  131.2 1.2 copy-done.1
  132.4 1.0 copy-done.8
  133.5 1.0 copy-done.9
  134.5 0.9 copy-done.10
  135.4 0.8 copy-done.20
  136.3 0.8 copy-done.21
  137.1 0.8 copy-done.22
  137.9 0.8 copy-done.23
  138.8 4.5 %shard_map.80 = (f32[2,1024,1024]{2,1,0:T(8,128)}, f32[2,128,128]{2,1,0:T(8,128)}) custom-call(f32[2,1024,1024]{2,1,0:T(8,128)} %get-tuple-element.37.core, f32[2,128,128]{2,1,0:T(8,128)S(1)} %copy-done.2, f32[2,128,128]{2,1,0:T(8,128)S(1)} %bitcast.1, f32[2,64,1024]{2,1,0:T(8,128)S(1)} %copy-done.8, ...), custom_call_target="tpu_custom_call", output_to_operand_aliasing={{0}: (0, {})} | custom-call | tf_op jit(solution)/shard_map/pallas_call | solution.py:432
  (29 shorter events, 1.9 us)
Async XLA Ops:
  0.6 35.4 %copy-start.5 = (bf16[4,256,256]{2,1,0:T(8,128)(2,1)S(1)}, bf16[4,256,256]{2,1,0:T(8,128)(2,1)}, u32[]{:S(2)}) copy-start(bf16[4,256,256]{2,1,0:T(8,128)(2,1)} %constant.2.clone.tab) | copy-start | bytes 1572868
  0.6 35.4 %copy-start.2 = (f32[2,128,128]{2,1,0:T(8,128)S(1)}, f32[2,128,128]{2,1,0:T(8,128)}, u32[]{:S(2)}) copy-start(f32[2,128,128]{2,1,0:T(8,128)} %ill.3) | copy-start | bytes 393220
  36.0 1.0 copy-start.6
  37.1 1.0 copy-start.7
  38.1 0.8 copy-start.16
  38.9 0.8 copy-start.17
  39.8 0.8 copy-start.18
  40.6 0.8 copy-start.19
  79.0 0.8 copy-start.3
  79.8 0.8 copy-start.4
  80.6 0.7 copy-start.11
  81.3 0.6 copy-start.12
  81.9 0.6 copy-start.13
  82.5 0.6 copy-start.14
  83.1 0.6 copy-start.15
  130.0 1.2 copy-start
  131.2 1.2 copy-start.1
  132.4 1.0 copy-start.8
  133.5 1.0 copy-start.9
  134.5 0.9 copy-start.10
  135.4 0.8 copy-start.20
  136.3 0.8 copy-start.21
  137.1 0.8 copy-start.22
  137.9 0.8 copy-start.23

commit v2 on v1

v2 whole, which is shorter than its diff:
```python
import functools
import math

import jax
import jax.numpy as jnp
import ml_dtypes
import numpy as np
from jax import lax
from jax.experimental import pallas as pl
from jax.experimental.pallas import tpu as pltpu
from jax.sharding import PartitionSpec as P

MESH = pl.DeviceIdType.MESH
PATCH = 128
HALF = 64
TILE = 1024
CAP = 64
LANE_TILES = TILE // PATCH
GROUP = 8
GROUP_FAR = 4
RING = 8
step_object = 0.25
DIRS = ((1, 0), (-1, 0), (0, 1), (0, -1), (1, 1), (1, -1), (-1, 1), (-1, -1))
SMALL_ROWS = 32
ANY = pl.BlockSpec(memory_space=pltpu.HBM)
IN_VMEM = pl.BlockSpec(memory_space=pltpu.VMEM)
IN_SMEM = pl.BlockSpec(memory_space=pltpu.SMEM)


def f32(*shape):
    return jax.ShapeDtypeStruct(shape, jnp.float32)


STRIPS = (
    f32(2, HALF, TILE), f32(2, HALF, TILE), f32(2, TILE // 2, PATCH), f32(2, TILE // 2, PATCH),
    f32(2, HALF, PATCH), f32(2, HALF, PATCH), f32(2, HALF, PATCH), f32(2, HALF, PATCH),
)


def tables():
    ids = np.arange(PATCH)
    angles = (np.outer(ids, ids) % PATCH) * (2 * math.pi / PATCH)
    cosine, sine = np.cos(angles) / math.sqrt(PATCH), np.sin(angles) / math.sqrt(PATCH)
    forward = np.block([[cosine, -sine], [sine, cosine]])
    out = []
    for matrix in (forward, forward.T):
        high = matrix.astype(np.float32).astype(ml_dtypes.bfloat16)
        out += [high, (matrix - high.astype(np.float64)).astype(np.float32).astype(ml_dtypes.bfloat16)]
    return np.stack(out)


def place():
    return lax.axis_index("row"), lax.axis_index("col"), lax.axis_size("row"), lax.axis_size("col")


def exists(da, db):
    a, b, rows, cols = place()
    return (a + da >= 0) & (a + da < rows) & (b + db >= 0) & (b + db < cols)


def strip_copy(d, src, dst, send_sem, recv_sem):
    a, b, _, _ = place()
    da, db = DIRS[d]
    return pltpu.make_async_remote_copy(
        src_ref=src, dst_ref=dst, send_sem=send_sem.at[d], recv_sem=recv_sem.at[d],
        device_id=(a + da, b + db), device_id_type=MESH,
    )


def start_strips(srcs, dsts, send_sem, recv_sem, which=range(8)):
    for d in which:
        da, db = DIRS[d]

        @pl.when(exists(da, db))
        def _():
            strip_copy(d, srcs[d], dsts[d], send_sem, recv_sem).start()


def wait_strips(srcs, dsts, send_sem, recv_sem):
    for d, (da, db) in enumerate(DIRS):
        @pl.when(exists(-da, -db))
        def _():
            strip_copy(d, srcs[d], dsts[d], send_sem, recv_sem).wait_recv()

        @pl.when(exists(da, db))
        def _():
            strip_copy(d, srcs[d], dsts[d], send_sem, recv_sem).wait_send()


def greet_strips(barrier, dirs):
    a, b, _, _ = place()
    for da, db in dirs:
        @pl.when(exists(da, db))
        def _():
            pl.semaphore_signal(barrier, inc=1, device_id=(a + da, b + db), device_id_type=MESH)


def folded(low_lanes, first, second):
    keep = (lax.broadcasted_iota(jnp.int32, first.shape, 1) < HALF) == low_lanes
    return jnp.where(keep, first, pltpu.roll(second, HALF, 1))


def split(x):
    high = x.astype(jnp.bfloat16)
    return high, (x - high.astype(jnp.float32)).astype(jnp.bfloat16)


def dot(x, y):
    return jnp.dot(x, y, preferred_element_type=jnp.float32)


def right(xs, high, low):
    parts = [split(x) for x in xs]
    both = dot(jnp.concatenate([half for part in parts for half in part], 0), high)
    rest = dot(jnp.concatenate([part[0] for part in parts], 0), low)
    n = xs[0].shape[0]
    return [both[2 * n * k:2 * n * k + n] + both[2 * n * k + n:2 * n * (k + 1)] + rest[n * k:n * (k + 1)] for k in range(len(xs))]


def left(high, low, x):
    xh, xl = split(x)
    return dot(high, xh) + dot(high, xl) + dot(low, xh)


def side_by_side(y):
    return jnp.concatenate([jnp.concatenate([y[:PATCH, c:c + PATCH], y[PATCH:, c:c + PATCH]], 1) for c in (0, PATCH)], 0)


def project(z, a):
    z_r, z_i = z[:PATCH], z[PATCH:]
    factor = a * jnp.minimum(lax.rsqrt(z_r * z_r + z_i * z_i), 2.0)
    return jnp.concatenate([factor * z_r, factor * z_i], 0)


def solve(waves, amps, tab):
    fh, fl, bh, bl = tab[0], tab[1], tab[2], tab[3]
    xs = [jnp.concatenate([jnp.concatenate(waves[k], 1) for k in (g, g + 1)], 0) for g in range(0, len(waves), 2)]
    ys = right(xs, fh, fl)
    qs = [project(left(bh, bl, side_by_side(y)), a) for y, a in zip(ys, amps)]
    ns = right([side_by_side(left(fh, fl, q)) for q in qs], bh, bl)
    return [(n[r:r + PATCH, :PATCH], n[r:r + PATCH, PATCH:]) for n in ns for r in (0, PATCH)]


def patch_wave(buf, ill, rows, ta, tb, shift, first):
    o_r = jnp.where(first, buf[0, ta, rows, :], buf[0, tb, rows, :])
    o_i = jnp.where(first, buf[1, ta, rows, :], buf[1, tb, rows, :])
    p_r, p_i = pltpu.roll(ill[0], shift, 1), pltpu.roll(ill[1], shift, 1)
    return (o_r, o_i, p_r, p_i), (p_r * o_r - p_i * o_i, p_r * o_i + p_i * o_r)


def gradients(parts, wave, new):
    o_r, o_i, p_r, p_i = parts
    c_r, c_i = new[0] - wave[0], new[1] - wave[1]
    terms = (p_r * c_r + p_i * c_i, p_r * c_i - p_i * c_r)
    return terms, (o_r * c_r + o_i * c_i, o_r * c_i - o_i * c_r)


def inside(row, column):
    return (row >= HALF) & (row <= TILE - HALF) & (column >= HALF) & (column <= TILE - HALF)


def early_kernel(pos, cnt, obj, ill, amp, tab, *refs):
    strips, terms, hout = refs[:8], refs[8], refs[9]
    ob, packed, staged, hacc, ampbuf, sem, asem, tsem, send_sem, recv_sem = refs[10:]
    a, b, rows, cols = place()
    count = cnt[0, 0]
    steps = CAP // GROUP
    barrier = pltpu.get_barrier_semaphore()
    greet_strips(barrier, DIRS)
    order = (LANE_TILES - 1, 0) + tuple(range(1, LANE_TILES - 1))
    reads = {
        (p, t): pltpu.make_async_copy(obj.at[p, :, t * PATCH:(t + 1) * PATCH], ob.at[p, t], sem.at[p * LANE_TILES + t])
        for t in order for p in range(2)
    }
    for copy in reads.values():
        copy.start()

    def amp_copy(i):
        return pltpu.make_async_copy(amp.at[0, 0, pl.ds(i * GROUP, GROUP)], ampbuf.at[i], asem.at[i])

    for i in range(steps):
        amp_copy(i).start()
    high = 1 + (a > 0).astype(jnp.int32) + (a < rows - 1).astype(jnp.int32)
    wide = 1 + (b > 0).astype(jnp.int32) + (b < cols - 1).astype(jnp.int32)
    pl.semaphore_wait(barrier, high * wide - 1)
    row_part = {1: slice(TILE - HALF, TILE), -1: slice(0, HALF), 0: slice(0, TILE)}
    col_part = {1: slice(TILE - PATCH, TILE), -1: slice(0, PATCH), 0: slice(0, TILE)}
    srcs = [obj.at[:, row_part[da], col_part[db]] for da, db in DIRS]
    srcs[2], srcs[3] = packed.at[0], packed.at[1]
    start_strips(srcs, strips, send_sem, recv_sem, (0, 1, 4, 5, 6, 7))
    half = TILE // 2
    for n, t in enumerate((LANE_TILES - 1, 0)):
        for p in range(2):
            reads[p, t].wait()
            packed[n, p] = folded(n == 1, ob[p, t, 0:half, :], ob[p, t, half:TILE, :])
        start_strips(srcs, strips, send_sem, recv_sem, (2 + n,))
    for p in range(2):
        ob[p, LANE_TILES] = jnp.zeros((TILE, PATCH), jnp.float32)
    hacc[...] = jnp.zeros_like(hacc)
    for t in order[2:]:
        for p in range(2):
            reads[p, t].wait()
    lane = lax.broadcasted_iota(jnp.int32, (PATCH, PATCH), 1)

    def term_copy(i):
        return pltpu.make_async_copy(staged.at[lax.rem(i, 2)], terms.at[pl.ds(i * GROUP, GROUP)], tsem.at[lax.rem(i, 2)])

    def step(i, carry):
        amp_copy(i).wait()
        info, waves = [], []
        for g in range(GROUP):
            s = i * GROUP + g
            row, column = pos[0, 0, s, 0], pos[0, 0, s, 1]
            good = inside(row, column) & (s < count)
            start = jnp.where(good, row - HALF, 0)
            at = jnp.where(good, column - HALF, 0)
            t, shift = at >> 7, at & (PATCH - 1)
            ta = jnp.where(good, t, LANE_TILES)
            tb = jnp.where(good, jnp.minimum(t + 1, LANE_TILES - 1), LANE_TILES)
            parts, wave = patch_wave(ob, ill, pl.ds(start, PATCH), ta, tb, shift, lane >= shift)
            info.append((parts, shift))
            waves.append(wave)
        amps = [jnp.concatenate([ampbuf[i, g], ampbuf[i, g + 1]], 1) for g in range(0, GROUP, 2)]
        news = solve(waves, amps, tab)

        @pl.when(i >= 2)
        def _():
            term_copy(i - 2).wait()
        for g in range(GROUP):
            parts, shift = info[g]
            out, h = gradients(parts, waves[g], news[g])
            for p in range(2):
                staged[lax.rem(i, 2), g, p] = out[p]
                hacc[p * PATCH:(p + 1) * PATCH] += pltpu.roll(h[p], PATCH - shift, 1)
        term_copy(i).start()
        return carry

    lax.fori_loop(0, steps, step, 0)
    hout[...] = hacc[...]
    for i in (steps - 2, steps - 1):
        term_copy(i).wait()
    wait_strips(srcs, strips, send_sem, recv_sem)


def run_early(positions, slot_counts, obj, ill, amplitudes, tab):
    dma = pltpu.SemaphoreType.DMA
    return pl.pallas_call(
        early_kernel,
        out_shape=STRIPS + (f32(CAP, 2, PATCH, PATCH), f32(2 * PATCH, PATCH)),
        in_specs=[IN_SMEM, IN_SMEM, ANY, IN_VMEM, ANY, IN_VMEM],
        out_specs=(ANY,) * 9 + (IN_VMEM,),
        scratch_shapes=[
            pltpu.VMEM((2, LANE_TILES + 1, TILE, PATCH), jnp.float32), pltpu.VMEM((2, 2, TILE // 2, PATCH), jnp.float32),
            pltpu.VMEM((2, GROUP, 2, PATCH, PATCH), jnp.float32), pltpu.VMEM((2 * PATCH, PATCH), jnp.float32),
            pltpu.VMEM((CAP // GROUP, GROUP, PATCH, PATCH), jnp.float32),
            dma((2 * LANE_TILES,)), dma((CAP // GROUP,)), dma((2,)), dma((8,)), dma((8,)),
        ],
        compiler_params=pltpu.CompilerParams(collective_id=0, has_side_effects=True, vmem_limit_bytes=58 * 2**20),
    )(positions, slot_counts, obj, ill, amplitudes, tab)


def border(d):
    da, db = DIRS[d]
    rows = {1: slice(0, HALF), -1: slice(HALF + TILE, 2 * HALF + TILE), 0: slice(HALF, HALF + TILE)}[da]
    return rows, {1: 0, -1: LANE_TILES + 1, 0: None}[db]


def border_views(buf, strip, d):
    rows, tile = border(d)
    if DIRS[d][0] == 0:
        return [(strip, buf.at[:, tile, HALF:HALF + TILE // 2, :])]
    if tile is not None:
        return [(strip, buf.at[:, tile, rows, :])]
    return [
        (strip.at[p, :, t * PATCH:(t + 1) * PATCH], buf.at[p, t + 1, rows, :])
        for p in range(2) for t in range(LANE_TILES)
    ]


def slots_kernel(pos, cnt, obj, ill, amp, tab, terms, hearly, *refs):
    halo, out, edges, hout = refs[:8], refs[8], refs[9:17], refs[17]
    ob, gr, hacc, ampbuf, held, near, far, sem, asem, tsem, osem = refs[18:]
    count = cnt[0, 0]
    body_copies = [
        pltpu.make_async_copy(obj.at[p, :, t * PATCH:(t + 1) * PATCH], ob.at[p, t + 1, HALF:HALF + TILE, :], sem.at[p * 8 + t])
        for p in range(2) for t in range(LANE_TILES)
    ]

    def listed(s, sizes):
        good = inside(pos[0, 0, s, 0], pos[0, 0, s, 1])

        @pl.when(good)
        def _():
            near[sizes[0]] = s

        @pl.when(jnp.logical_not(good))
        def _():
            far[sizes[1]] = s
        step = good.astype(jnp.int32)
        return sizes[0] + step, sizes[1] + 1 - step

    n_near, n_far = lax.fori_loop(0, count, listed, (jnp.int32(0), jnp.int32(0)))

    def term_copy(j):
        return pltpu.make_async_copy(terms.at[near[j]], held.at[lax.rem(j, RING)], tsem.at[lax.rem(j, RING)])

    def amp_copy(j):
        return pltpu.make_async_copy(amp.at[0, 0, far[j]], ampbuf.at[j], asem.at[j])

    @pl.loop(0, jnp.minimum(n_near, RING))
    def _(j):
        term_copy(j).start()

    @pl.loop(0, n_far)
    def _(j):
        amp_copy(j).start()

    for copy in body_copies:
        copy.start()
    halo_copies = []
    for d in range(8):
        views = border_views(ob, halo[d], d)
        halo_copies.append([pltpu.make_async_copy(src, dst, osem.at[d, n]) for n, (src, dst) in enumerate(views)])
    for d, (da, db) in enumerate(DIRS):
        @pl.when(exists(-da, -db))
        def _():
            for copy in halo_copies[d]:
                copy.start()

        @pl.when(jnp.logical_not(exists(-da, -db)))
        def _():
            rows, tile = border(d)
            for p in range(2):
                for t in range(1, LANE_TILES + 1) if tile is None else (tile,):
                    ob[p, t, rows, :] = jnp.zeros((rows.stop - rows.start, PATCH), jnp.float32)

    zero = jnp.zeros((PATCH, PATCH), jnp.float32)

    @pl.loop(0, (TILE + PATCH) // PATCH)
    def _(i):
        rows = pl.ds(pl.multiple_of(i * PATCH, PATCH), PATCH)
        for p in range(2):
            for t in range(LANE_TILES + 2):
                gr[p, t, rows, :] = zero
            ob[p, LANE_TILES + 2, rows, :] = zero
    hacc[...] = hearly[...]
    lane = lax.broadcasted_iota(jnp.int32, (PATCH, PATCH), 1)

    def add(rows, t, first, term):
        for p in range(2):
            now = jnp.where(first, gr[p, t, rows, :], gr[p, t + 1, rows, :]) + term[p]
            pltpu.store(gr.at[p, t, rows, :], now, mask=first)
            pltpu.store(gr.at[p, t + 1, rows, :], now, mask=jnp.logical_not(first))

    @pl.loop(0, n_near)
    def _(j):
        s = near[j]
        term_copy(j).wait()
        column = pos[0, 0, s, 1] + HALF
        add(pl.ds(pos[0, 0, s, 0], PATCH), column >> 7, lane >= (column & (PATCH - 1)), [held[lax.rem(j, RING), p] for p in range(2)])

        @pl.when(j + RING < n_near)
        def _():
            term_copy(j + RING).start()

    for copy in body_copies:
        copy.wait()
    for d, (da, db) in enumerate(DIRS):
        @pl.when(exists(-da, -db))
        def _():
            for copy in halo_copies[d]:
                copy.wait()
            if da == 0:
                tile = border(d)[1]
                for p in range(2):
                    ob[p, tile, HALF + TILE // 2:HALF + TILE, :] = pltpu.roll(ob[p, tile, HALF:HALF + TILE // 2, :], HALF, 1)

    @pl.loop(0, n_far)
    def _(j):
        amp_copy(j).wait()

    def step(i, carry):
        info, waves, slots = [], [], []
        for g in range(GROUP_FAR):
            live = i * GROUP_FAR + g < n_far
            j = jnp.where(live, i * GROUP_FAR + g, 0)
            s = far[j]
            rows = pl.ds(pos[0, 0, s, 0], PATCH)
            column = pos[0, 0, s, 1] + HALF
            t, shift = column >> 7, column & (PATCH - 1)
            first = lane >= shift
            ta, tb = jnp.where(live, t, LANE_TILES + 2), jnp.where(live, t + 1, LANE_TILES + 2)
            parts, wave = patch_wave(ob, ill, rows, ta, tb, shift, first)
            info.append((rows, t, shift, first, parts))
            waves.append(wave)
            slots.append(j)
        amps = [jnp.concatenate([ampbuf[slots[g]], ampbuf[slots[g + 1]]], 1) for g in range(0, GROUP_FAR, 2)]
        news = solve(waves, amps, tab)
        for g in range(GROUP_FAR):
            rows, t, shift, first, parts = info[g]
            term, h = gradients(parts, waves[g], news[g])
            add(rows, t, first, term)
            for p in range(2):
                hacc[p * PATCH:(p + 1) * PATCH] += pltpu.roll(h[p], PATCH - shift, 1)
        return carry

    lax.fori_loop(0, (n_far + GROUP_FAR - 1) // GROUP_FAR, step, 0)
    hout[...] = hacc[...]
    last = []
    for tile in (0, LANE_TILES + 1):
        for p in range(2):
            gr[p, tile, HALF:HALF + TILE // 2, :] = folded(
                tile > 0, gr[p, tile, HALF:HALF + TILE // 2, :], gr[p, tile, HALF + TILE // 2:HALF + TILE, :])
    for d in range(8):
        da, db = DIRS[d]
        views = border_views(gr, edges[d], DIRS.index((-da, -db)))
        last += [pltpu.make_async_copy(dst, src, osem.at[d, n]) for n, (src, dst) in enumerate(views)]
    for copy in last:
        copy.start()
    for p in range(2):
        for t in range(LANE_TILES):
            @pl.loop(0, TILE // PATCH)
            def _(i):
                rows = pl.ds(pl.multiple_of(HALF + i * PATCH, HALF), PATCH)
                ob[p, t + 1, rows, :] += step_object * gr[p, t + 1, rows, :]
            copy = pltpu.make_async_copy(
                ob.at[p, t + 1, HALF:HALF + TILE, :], out.at[p, :, t * PATCH:(t + 1) * PATCH], sem.at[p * 8 + t])
            copy.start()
            last.append(copy)
    for copy in last:
        copy.wait()


def run_slots(positions, slot_counts, obj, ill, amplitudes, tab, terms, hearly, halo):
    dma = pltpu.SemaphoreType.DMA
    return pl.pallas_call(
        slots_kernel,
        out_shape=(f32(2, TILE, TILE),) + STRIPS + (f32(2 * PATCH, PATCH),),
        in_specs=[IN_SMEM, IN_SMEM, ANY, IN_VMEM, ANY, IN_VMEM, ANY, IN_VMEM] + [ANY] * 8,
        out_specs=(ANY,) * 9 + (IN_VMEM,),
        scratch_shapes=[
            pltpu.VMEM((2, LANE_TILES + 3, TILE + PATCH, PATCH), jnp.float32),
            pltpu.VMEM((2, LANE_TILES + 2, TILE + PATCH, PATCH), jnp.float32),
            pltpu.VMEM((2 * PATCH, PATCH), jnp.float32), pltpu.VMEM((CAP, PATCH, PATCH), jnp.float32),
            pltpu.VMEM((RING, 2, PATCH, PATCH), jnp.float32), pltpu.SMEM((CAP,), jnp.int32), pltpu.SMEM((CAP,), jnp.int32),
            dma((16,)), dma((CAP,)), dma((RING,)), dma((8, 16)),
        ],
        compiler_params=pltpu.CompilerParams(vmem_limit_bytes=58 * 2**20),
    )(positions, slot_counts, obj, ill, amplitudes, tab, terms, hearly, *halo)


def return_kernel(h, *refs):
    edges, strips, total = refs[:8], refs[8:16], refs[16]
    pieces, sums, gathered, send_sem, recv_sem, s1, r1, s2, r2, s3, r3 = refs[17:]
    a, b, rows, cols = place()
    barrier = pltpu.get_barrier_semaphore()
    greet_strips(barrier, DIRS[4:])

    def col_peer(k):
        return lax.rem(b + k, cols)

    def row_peer(k):
        return lax.rem(a + k, rows)

    for k in range(1, rows):
        pl.semaphore_signal(barrier, inc=1, device_id=(row_peer(k), b), device_id_type=MESH)
    for k in range(1, cols):
        pl.semaphore_signal(barrier, inc=1, device_id=(a, col_peer(k)), device_id_type=MESH)
    high = (a > 0).astype(jnp.int32) + (a < rows - 1).astype(jnp.int32)
    wide = (b > 0).astype(jnp.int32) + (b < cols - 1).astype(jnp.int32)
    pl.semaphore_wait(barrier, cols - 1 + rows - 1 + high * wide)

    def piece_rows(k):
        return pl.ds(pl.multiple_of(k * SMALL_ROWS, SMALL_ROWS), SMALL_ROWS)

    def scatter(peer, slot):
        return pltpu.make_async_remote_copy(
            src_ref=h.at[piece_rows(peer)], dst_ref=pieces.at[slot], send_sem=s1.at[peer], recv_sem=r1.at[slot],
            device_id=(peer, b), device_id_type=MESH)

    def share(peer, slot):
        return pltpu.make_async_remote_copy(
            src_ref=sums.at[slot], dst_ref=sums.at[slot], send_sem=s2.at[peer], recv_sem=r2.at[slot],
            device_id=(a, peer), device_id_type=MESH)

    def gather(peer, slot):
        return pltpu.make_async_remote_copy(
            src_ref=gathered.at[slot], dst_ref=gathered.at[slot], send_sem=s3.at[peer], recv_sem=r3.at[slot],
            device_id=(peer, b), device_id_type=MESH)

    for k in range(1, rows):
        scatter(row_peer(k), a).start()
    start_strips(edges, strips, send_sem, recv_sem)
    pieces[a] = h[piece_rows(a), :]
    for k in range(1, rows):
        scatter(a, row_peer(k)).wait_recv()
    sums[b] = jnp.sum(pieces[...], axis=0)
    for k in range(1, cols):
        share(col_peer(k), b).start()
    for k in range(1, cols):
        share(b, col_peer(k)).wait_recv()
    gathered[a] = jnp.sum(sums[...], axis=0)
    for k in range(1, rows):
        gather(row_peer(k), a).start()
    for k in range(1, rows):
        gather(a, row_peer(k)).wait_recv()
    total[...] = gathered[...]
    for k in range(1, rows):
        scatter(row_peer(k), a).wait_send()
        gather(row_peer(k), a).wait_send()
    for k in range(1, cols):
        share(col_peer(k), b).wait_send()
    wait_strips(edges, strips, send_sem, recv_sem)


def return_edges(h, edges):
    rows, cols = lax.axis_size("row"), lax.axis_size("col")
    dma = pltpu.SemaphoreType.DMA
    return pl.pallas_call(
        return_kernel,
        out_shape=STRIPS + (f32(rows, SMALL_ROWS, PATCH),),
        in_specs=[IN_VMEM] + [ANY] * 8,
        out_specs=(ANY,) * 8 + (IN_VMEM,),
        scratch_shapes=[
            pltpu.VMEM((rows, SMALL_ROWS, PATCH), jnp.float32), pltpu.VMEM((cols, SMALL_ROWS, PATCH), jnp.float32),
            pltpu.VMEM((rows, SMALL_ROWS, PATCH), jnp.float32), dma((8,)), dma((8,)),
            dma((rows,)), dma((rows,)), dma((cols,)), dma((cols,)), dma((rows,)), dma((rows,)),
        ],
        compiler_params=pltpu.CompilerParams(collective_id=1, has_side_effects=True, vmem_limit_bytes=58 * 2**20),
    )(h, *edges)


def finish_kernel(rate, core, ill, total, *refs):
    strips, out, probe = refs[:8], refs[8], refs[9]
    top, bottom, west, east, sem, strip_sem = refs[10:16]
    held = refs[16:]
    middle = slice(HALF, TILE - HALF)
    parts = (
        (top, out.at[:, 0:HALF, :]), (bottom, out.at[:, TILE - HALF:TILE, :]),
        (west, out.at[:, middle, 0:PATCH]), (east, out.at[:, middle, TILE - PATCH:TILE]),
    )
    reads = [pltpu.make_async_copy(hbm, vmem, sem.at[n]) for n, (vmem, hbm) in enumerate(parts)]
    writes = [pltpu.make_async_copy(vmem, hbm, sem.at[n]) for n, (vmem, hbm) in enumerate(parts)]
    fetches = [pltpu.make_async_copy(strips[d], held[d], strip_sem.at[d]) for d in range(8)]
    for copy in reads:
        copy.start()
    for d, (da, db) in enumerate(DIRS):
        @pl.when(exists(-da, -db))
        def _():
            fetches[d].start()
    probe[...] = ill[...] + rate * total[...]
    for copy in reads:
        copy.wait()
    half = TILE // 2
    for d, (da, db) in enumerate(DIRS):
        @pl.when(exists(-da, -db))
        def _():
            fetches[d].wait()
            if da != 0:
                target = top if da > 0 else bottom
                cols = {0: slice(0, TILE), 1: slice(0, PATCH), -1: slice(TILE - PATCH, TILE)}[db]
                target[:, :, cols] += step_object * held[d][...]
            else:
                side = west if db > 0 else east
                cols = slice(0, PATCH) if db > 0 else slice(TILE - PATCH, TILE)
                low = lax.broadcasted_iota(jnp.int32, (half, PATCH), 1) < HALF
                keep = low if db > 0 else jnp.logical_not(low)
                for p in range(2):
                    first = jnp.where(keep, step_object * held[d][p], 0.0)
                    second = jnp.where(keep, pltpu.roll(step_object * held[d][p], HALF, 1), 0.0)
                    top[p, :, cols] += first[0:HALF]
                    side[p, 0:half - HALF, :] += first[HALF:half]
                    side[p, half - HALF:TILE - PATCH, :] += second[0:half - HALF]
                    bottom[p, :, cols] += second[half - HALF:half]
    for copy in writes:
        copy.start()
    for copy in writes:
        copy.wait()


def finish(core, ill, total, strips):
    rate = (CAP * lax.axis_size("row") * lax.axis_size("col")) ** (-0.5)
    return pl.pallas_call(
        functools.partial(finish_kernel, rate),
        out_shape=(f32(2, TILE, TILE), f32(2, PATCH, PATCH)),
        in_specs=[ANY, IN_VMEM, IN_VMEM] + [ANY] * 8,
        out_specs=(ANY, IN_VMEM),
        input_output_aliases={0: 0},
        scratch_shapes=[
            pltpu.VMEM((2, HALF, TILE), jnp.float32), pltpu.VMEM((2, HALF, TILE), jnp.float32),
            pltpu.VMEM((2, TILE - PATCH, PATCH), jnp.float32), pltpu.VMEM((2, TILE - PATCH, PATCH), jnp.float32),
            pltpu.SemaphoreType.DMA((4,)), pltpu.SemaphoreType.DMA((8,)),
        ] + [pltpu.VMEM(strip.shape, jnp.float32) for strip in STRIPS],
        compiler_params=pltpu.CompilerParams(vmem_limit_bytes=58 * 2**20),
    )(core, ill, total.reshape(2, PATCH, PATCH), *strips)


def shards(object_field, illumination, positions, slot_counts, amplitudes):
    shared = (positions, slot_counts, object_field, illumination, amplitudes, jnp.asarray(tables()))
    *halo, terms, hearly = run_early(*shared)
    core, *rest = run_slots(*shared, terms, hearly, halo)
    edges, h = rest[:8], rest[8]
    *strips, total = return_edges(h, edges)
    return finish(core, illumination, total, strips)


def solution(mesh):
    placed = (
        P(None, "row", "col"),
        P(),
        P("row", "col", None, None),
        P("row", "col"),
        P("row", "col", None, None, None),
    )
    return jax.shard_map(
        shards, mesh=mesh, in_specs=placed, out_specs=(P(None, "row", "col"), P()), check_vma=False
    )
```

time: 146 us -> 105 us (0.72)
  Pallas kernels: 122 us -> 101 us
  local copies, waits for them, and re-layouts: 19.7 us -> 1.37 us
    unnamed x49 -> x1, local copies, waits for them, and re-layouts: 19.7 us -> 1.37 us
    pallas_call x1, Pallas kernels: 37.5 us -> 24.2 us  [run_slots(): pl.pallas_call(slots_kernel, out_shape=(f32(2, TILE, TILE),) + STRIPS + (...]
    pallas_call x2, Pallas kernels: 80.1 us -> 70.4 us  [the longest x1 38 us: return_edges(): pl.pallas_call(return_kernel, out_shape=STRIPS + (f32(rows, SMALL_ROWS, P...]
    pallas_call x1, Pallas kernels: 4.5 us -> 6.03 us  [finish(): pl.pallas_call(functools.partial(finish_kernel, rate), out_shape=(f32(2,...]
where the time goes in v2:
time: 105 us; the launch traced here: 103 us
  Pallas kernels  101 us (96%)
  local copies, waits for them, and re-layouts  1.37 us (1%)
  between operations  1.3 us (1%)
    pallas_call x1, Pallas kernels, return_edges(): pl.pallas_call(return_kernel, out_shape=STRIPS + (f32(rows, SMALL_ROWS, P...  38 us
    pallas_call x1, Pallas kernels, run_early(): pl.pallas_call(early_kernel, out_shape=STRIPS + (f32(CAP, 2, PATCH, PATCH...  32.4 us
    pallas_call x1, Pallas kernels, run_slots(): pl.pallas_call(slots_kernel, out_shape=(f32(2, TILE, TILE),) + STRIPS + (...  24.2 us
    pallas_call x1, Pallas kernels, finish(): pl.pallas_call(functools.partial(finish_kernel, rate), out_shape=(f32(2,...  6.03 us

profile of v2, /device:TPU:6, one launch (start us, length us, event | category | flops | bytes accessed | tf_op | source)
XLA Modules:
  0.0 103.3 jit_solution(5034117707301260971)
XLA Ops:
  1.3 1.4 %copy.10.pos = s32[1,1,64,2]{3,2,1,0:T(8,128)} copy(s32[1,1,64,2]{2,3,1,0:T(2,128)} %param.8) | data formatting | bytes 1024 | tf_op args[2]
  2.6 32.4 %shard_map.77 = (f32[2,64,1024]{2,1,0:T(8,128)}, f32[2,64,1024]{2,1,0:T(8,128)}, f32[2,512,128]{2,1,0:T(8,128)}, f32[2,512,128]{2,1,0:T(8,128)}, f32[2,64,128]{2...) custom-call(s32[1,1,64,2]{3,2,1,0:T(8,128)} %copy.10.pos, ...), custom_call_target="tpu_custom_call" | custom-call | tf_op jit(solution)/shard_map/pallas_call | solution.py:247
  35.0 24.2 %shard_map.78 = (f32[2,1024,1024]{2,1,0:T(8,128)}, f32[2,64,1024]{2,1,0:T(8,128)}, f32[2,64,1024]{2,1,0:T(8,128)}, f32[2,512,128]{2,1,0:T(8,128)}, f32[2,512,128...) custom-call(s32[1,1,64,2]{3,2,1,0:T(8,128)} %copy.10.pos, ...), custom_call_target="tpu_custom_call" | custom-call | tf_op jit(solution)/shard_map/pallas_call | solution.py:436
  59.2 38.0 %shard_map.79 = (f32[2,64,1024]{2,1,0:T(8,128)}, f32[2,64,1024]{2,1,0:T(8,128)}, f32[2,512,128]{2,1,0:T(8,128)}, f32[2,512,128]{2,1,0:T(8,128)}, f32[2,64,128]{2...) custom-call(f32[256,128]{1,0:T(8,128)} %get-tuple-element.42.h, ...), custom_call_target="tpu_custom_call" | custom-call | tf_op jit(solution)/shard_map/pallas_call | solution.py:519
  97.2 6.0 %shard_map.80 = (f32[2,1024,1024]{2,1,0:T(8,128)}, f32[2,128,128]{2,1,0:T(8,128)}) custom-call(f32[2,1024,1024]{2,1,0:T(8,128)} %get-tuple-element.41.core, f32[2,128,128]{2,1,0:T(8,128)} %ill.5, f32[2,128,128]{2,1,0:T(8,128)} %bitcast.1, f32[2,64,1024]{2,1,0:T(8,128)} %get-tuple-element.52.refs_0_, ...), custom_call_target="tpu_custom_call", output_to_operand_aliasing={{0}: (0, {})} | custom-call | tf_op jit(solution)/shard_map/pallas_call | solution.py:583

commit v3 on v2

--- a/solution.py
+++ b/solution.py
@@ -16,12 +16,14 @@
 TILE = 1024
 CAP = 64
 LANE_TILES = TILE // PATCH
-GROUP = 8
+GROUP = 16
 GROUP_FAR = 4
+CHUNKS = 4
+PACE = (0, 0, 1, 2, 4)
 RING = 8
 step_object = 0.25
 DIRS = ((1, 0), (-1, 0), (0, 1), (0, -1), (1, 1), (1, -1), (-1, 1), (-1, -1))
-SMALL_ROWS = 32
+SMALL_ROWS = 16
 ANY = pl.BlockSpec(memory_space=pltpu.HBM)
 IN_VMEM = pl.BlockSpec(memory_space=pltpu.VMEM)
 IN_SMEM = pl.BlockSpec(memory_space=pltpu.SMEM)
@@ -76,8 +78,10 @@
             strip_copy(d, srcs[d], dsts[d], send_sem, recv_sem).start()
 
 
-def wait_strips(srcs, dsts, send_sem, recv_sem):
-    for d, (da, db) in enumerate(DIRS):
+def wait_strips(srcs, dsts, send_sem, recv_sem, which=range(8)):
+    for d in which:
+        da, db = DIRS[d]
+
         @pl.when(exists(-da, -db))
         def _():
             strip_copy(d, srcs[d], dsts[d], send_sem, recv_sem).wait_recv()
@@ -134,11 +138,22 @@
 
 def solve(waves, amps, tab):
     fh, fl, bh, bl = tab[0], tab[1], tab[2], tab[3]
-    xs = [jnp.concatenate([jnp.concatenate(waves[k], 1) for k in (g, g + 1)], 0) for g in range(0, len(waves), 2)]
-    ys = right(xs, fh, fl)
-    qs = [project(left(bh, bl, side_by_side(y)), a) for y, a in zip(ys, amps)]
-    ns = right([side_by_side(left(fh, fl, q)) for q in qs], bh, bl)
-    return [(n[r:r + PATCH, :PATCH], n[r:r + PATCH, PATCH:]) for n in ns for r in (0, PATCH)]
+    pairs = range(len(waves) // 2)
+    held = [jnp.concatenate([jnp.concatenate(waves[k], 1) for k in (2 * p, 2 * p + 1)], 0) for p in pairs]
+    cut = len(pairs) // 2
+    for tick in range(5):
+        for stage, part in ((tick, list(pairs[:cut])), (tick - 1, list(pairs[cut:]))):
+            if stage in (0, 3):
+                done = right([held[p] for p in part], *((fh, fl) if stage == 0 else (bh, bl)))
+            elif stage == 1:
+                done = [project(left(bh, bl, side_by_side(held[p])), amps[p]) for p in part]
+            elif stage == 2:
+                done = [side_by_side(left(fh, fl, held[p])) for p in part]
+            else:
+                continue
+            for p, value in zip(part, done):
+                held[p] = value
+    return [(n[r:r + PATCH, :PATCH], n[r:r + PATCH, PATCH:]) for n in held for r in (0, PATCH)]
 
 
 def patch_wave(buf, ill, rows, ta, tb, shift, first):
@@ -210,7 +225,7 @@
         info, waves = [], []
         for g in range(GROUP):
             s = i * GROUP + g
-            row, column = pos[0, 0, s, 0], pos[0, 0, s, 1]
+            row, column = pos[0, 0, 0, s], pos[0, 0, 1, s]
             good = inside(row, column) & (s < count)
             start = jnp.where(good, row - HALF, 0)
             at = jnp.where(good, column - HALF, 0)
@@ -287,7 +302,7 @@
     ]
 
     def listed(s, sizes):
-        good = inside(pos[0, 0, s, 0], pos[0, 0, s, 1])
+        good = inside(pos[0, 0, 0, s], pos[0, 0, 1, s])
 
         @pl.when(good)
         def _():
@@ -356,8 +371,8 @@
     def _(j):
         s = near[j]
         term_copy(j).wait()
-        column = pos[0, 0, s, 1] + HALF
-        add(pl.ds(pos[0, 0, s, 0], PATCH), column >> 7, lane >= (column & (PATCH - 1)), [held[lax.rem(j, RING), p] for p in range(2)])
+        column = pos[0, 0, 1, s] + HALF
+        add(pl.ds(pos[0, 0, 0, s], PATCH), column >> 7, lane >= (column & (PATCH - 1)), [held[lax.rem(j, RING), p] for p in range(2)])
 
         @pl.when(j + RING < n_near)
         def _():
@@ -385,8 +400,8 @@
             live = i * GROUP_FAR + g < n_far
             j = jnp.where(live, i * GROUP_FAR + g, 0)
             s = far[j]
-            rows = pl.ds(pos[0, 0, s, 0], PATCH)
-            column = pos[0, 0, s, 1] + HALF
+            rows = pl.ds(pos[0, 0, 0, s], PATCH)
+            column = pos[0, 0, 1, s] + HALF
             t, shift = column >> 7, column & (PATCH - 1)
             first = lane >= shift
             ta, tb = jnp.where(live, t, LANE_TILES + 2), jnp.where(live, t + 1, LANE_TILES + 2)
@@ -451,80 +466,120 @@
 
 def return_kernel(h, *refs):
     edges, strips, total = refs[:8], refs[8:16], refs[16]
-    pieces, sums, gathered, send_sem, recv_sem, s1, r1, s2, r2, s3, r3 = refs[17:]
+    other, mine, pieces, sums, gathered, send_sem, recv_sem, s0, r0, s1, r1, s2, r2, s3, r3 = refs[17:]
     a, b, rows, cols = place()
+    chips = cols // 2
+    q, core = b // 2, lax.rem(b, 2)
+    partner = (a, b + 1 - 2 * core)
+
+    def row_peer(k):
+        return lax.rem(a + k, rows)
+
+    def chip_peer(k):
+        return lax.rem(q + k, chips)
+
     barrier = pltpu.get_barrier_semaphore()
     greet_strips(barrier, DIRS[4:])
-
-    def col_peer(k):
-        return lax.rem(b + k, cols)
-
-    def row_peer(k):
-        return lax.rem(a + k, rows)
-
+    pl.semaphore_signal(barrier, inc=1, device_id=partner, device_id_type=MESH)
     for k in range(1, rows):
         pl.semaphore_signal(barrier, inc=1, device_id=(row_peer(k), b), device_id_type=MESH)
-    for k in range(1, cols):
-        pl.semaphore_signal(barrier, inc=1, device_id=(a, col_peer(k)), device_id_type=MESH)
+    for k in range(1, chips):
+        pl.semaphore_signal(barrier, inc=1, device_id=(a, chip_peer(k) * 2 + core), device_id_type=MESH)
+    across = ((core == 1) & (b < cols - 1)) | ((core == 0) & (b > 0))
+    side = b + 2 * core - 1
+
+    @pl.when(across)
+    def _():
+        pl.semaphore_signal(barrier, inc=1, device_id=(a, side), device_id_type=MESH)
     high = (a > 0).astype(jnp.int32) + (a < rows - 1).astype(jnp.int32)
     wide = (b > 0).astype(jnp.int32) + (b < cols - 1).astype(jnp.int32)
-    pl.semaphore_wait(barrier, cols - 1 + rows - 1 + high * wide)
+    pl.semaphore_wait(barrier, 1 + rows - 1 + chips - 1 + across.astype(jnp.int32) + high * wide)
 
     def piece_rows(k):
         return pl.ds(pl.multiple_of(k * SMALL_ROWS, SMALL_ROWS), SMALL_ROWS)
 
+    def half_rows(k):
+        return pl.ds(pl.multiple_of(k * PATCH, PATCH), PATCH)
+
+    def remote(src, dst, send, recv, device):
+        return pltpu.make_async_remote_copy(
+            src_ref=src, dst_ref=dst, send_sem=send, recv_sem=recv, device_id=device, device_id_type=MESH)
+
+    def swap():
+        return remote(h.at[half_rows(1 - core)], other, s0.at[0], r0.at[0], partner)
+
     def scatter(peer, slot):
-        return pltpu.make_async_remote_copy(
-            src_ref=h.at[piece_rows(peer)], dst_ref=pieces.at[slot], send_sem=s1.at[peer], recv_sem=r1.at[slot],
-            device_id=(peer, b), device_id_type=MESH)
+        return remote(mine.at[piece_rows(peer)], pieces.at[slot], s1.at[peer], r1.at[slot], (peer, b))
 
     def share(peer, slot):
-        return pltpu.make_async_remote_copy(
-            src_ref=sums.at[slot], dst_ref=sums.at[slot], send_sem=s2.at[peer], recv_sem=r2.at[slot],
-            device_id=(a, peer), device_id_type=MESH)
+        return remote(sums.at[slot], sums.at[slot], s2.at[peer], r2.at[slot], (a, peer * 2 + core))
 
     def gather(peer, slot):
-        return pltpu.make_async_remote_copy(
-            src_ref=gathered.at[slot], dst_ref=gathered.at[slot], send_sem=s3.at[peer], recv_sem=r3.at[slot],
-            device_id=(peer, b), device_id_type=MESH)
-
+        return remote(gathered.at[core, slot], gathered.at[core, slot], s3.at[peer], r3.at[slot], (peer, b))
+
+    def hand(which):
+        return remote(gathered.at[which], gathered.at[which], s0.at[1], r0.at[1], partner)
+
+    def parts(refs, c):
+        return [
+            ref if d >= 4 else ref.at[:, c * (HALF // CHUNKS):(c + 1) * (HALF // CHUNKS), :] if d < 2
+            else ref.at[:, c * (TILE // 2 // CHUNKS):(c + 1) * (TILE // 2 // CHUNKS), :]
+            for d, ref in enumerate(refs)
+        ]
+
+    def send_strips(stage):
+        for c in range(PACE[stage], PACE[stage + 1]):
+            start_strips(parts(edges, c), parts(strips, c), send_sem.at[c], recv_sem.at[c], range(8) if c == 0 else range(4))
+
+    swap().start()
+    send_strips(0)
+    swap().wait_recv()
+    mine[...] = h[half_rows(core), :] + other[...]
     for k in range(1, rows):
         scatter(row_peer(k), a).start()
-    start_strips(edges, strips, send_sem, recv_sem)
-    pieces[a] = h[piece_rows(a), :]
+    send_strips(1)
+    pieces[a] = mine[piece_rows(a), :]
     for k in range(1, rows):
         scatter(a, row_peer(k)).wait_recv()
-    sums[b] = jnp.sum(pieces[...], axis=0)
-    for k in range(1, cols):
-        share(col_peer(k), b).start()
-    for k in range(1, cols):
-        share(b, col_peer(k)).wait_recv()
-    gathered[a] = jnp.sum(sums[...], axis=0)
+    sums[q] = jnp.sum(pieces[...], axis=0)
+    for k in range(1, chips):
+        share(chip_peer(k), q).start()
+    send_strips(2)
+    for k in range(1, chips):
+        share(q, chip_peer(k)).wait_recv()
+    gathered[core, a] = jnp.sum(sums[...], axis=0)
     for k in range(1, rows):
         gather(row_peer(k), a).start()
+    send_strips(3)
     for k in range(1, rows):
         gather(a, row_peer(k)).wait_recv()
+    hand(core).start()
+    hand(1 - core).wait_recv()
     total[...] = gathered[...]
+    swap().wait_send()
+    hand(core).wait_send()
     for k in range(1, rows):
         scatter(row_peer(k), a).wait_send()
         gather(row_peer(k), a).wait_send()
-    for k in range(1, cols):
-        share(col_peer(k), b).wait_send()
-    wait_strips(edges, strips, send_sem, recv_sem)
+    for k in range(1, chips):
+        share(chip_peer(k), q).wait_send()
+    for c in range(CHUNKS):
+        wait_strips(parts(edges, c), parts(strips, c), send_sem.at[c], recv_sem.at[c], range(8) if c == 0 else range(4))
 
 
 def return_edges(h, edges):
-    rows, cols = lax.axis_size("row"), lax.axis_size("col")
+    rows, chips = lax.axis_size("row"), lax.axis_size("col") // 2
     dma = pltpu.SemaphoreType.DMA
     return pl.pallas_call(
         return_kernel,
-        out_shape=STRIPS + (f32(rows, SMALL_ROWS, PATCH),),
+        out_shape=STRIPS + (f32(2, rows, SMALL_ROWS, PATCH),),
         in_specs=[IN_VMEM] + [ANY] * 8,
         out_specs=(ANY,) * 8 + (IN_VMEM,),
         scratch_shapes=[
-            pltpu.VMEM((rows, SMALL_ROWS, PATCH), jnp.float32), pltpu.VMEM((cols, SMALL_ROWS, PATCH), jnp.float32),
-            pltpu.VMEM((rows, SMALL_ROWS, PATCH), jnp.float32), dma((8,)), dma((8,)),
-            dma((rows,)), dma((rows,)), dma((cols,)), dma((cols,)), dma((rows,)), dma((rows,)),
+            pltpu.VMEM((PATCH, PATCH), jnp.float32), pltpu.VMEM((PATCH, PATCH), jnp.float32),
+            pltpu.VMEM((rows, SMALL_ROWS, PATCH), jnp.float32), pltpu.VMEM((chips, SMALL_ROWS, PATCH), jnp.float32),
+            pltpu.VMEM((2, rows, SMALL_ROWS, PATCH), jnp.float32), dma((CHUNKS, 8)), dma((CHUNKS, 8)),
+            dma((2,)), dma((2,)), dma((rows,)), dma((rows,)), dma((chips,)), dma((chips,)), dma((rows,)), dma((rows,)),
         ],
         compiler_params=pltpu.CompilerParams(collective_id=1, has_side_effects=True, vmem_limit_bytes=58 * 2**20),
     )(h, *edges)
@@ -596,7 +651,7 @@
 
 
 def shards(object_field, illumination, positions, slot_counts, amplitudes):
-    shared = (positions, slot_counts, object_field, illumination, amplitudes, jnp.asarray(tables()))
+    shared = (jnp.swapaxes(positions, 2, 3), slot_counts, object_field, illumination, amplitudes, jnp.asarray(tables()))
     *halo, terms, hearly = run_early(*shared)
     core, *rest = run_slots(*shared, terms, hearly, halo)
     edges, h = rest[:8], rest[8]

time: 105 us -> 95.1 us (0.906); the launches traced: 103 us -> 94.9 us
  Pallas kernels: 101 us -> 93.6 us
  local copies, waits for them, and re-layouts: 1.37 us -> 0 us
    pallas_call x1, Pallas kernels: 24.2 us -> 15.5 us  [run_slots(): pl.pallas_call(slots_kernel, out_shape=(f32(2, TILE, TILE),) + STRIPS + (...]
    pallas_call x1, Pallas kernels: 38 us -> 39.7 us  [return_edges(): pl.pallas_call(return_kernel, out_shape=STRIPS + (f32(2, rows, SMALL_ROWS...]
    unnamed x1 -> x0, local copies, waits for them, and re-layouts: 1.37 us -> none
where the time goes in v3:
time: 95.1 us; the launch traced here: 94.9 us
  Pallas kernels  93.6 us (98%)
  between operations  1.3 us (1%)
    pallas_call x1, Pallas kernels, return_edges(): pl.pallas_call(return_kernel, out_shape=STRIPS + (f32(2, rows, SMALL_ROWS...  39.7 us
    pallas_call x1, Pallas kernels, run_early(): pl.pallas_call(early_kernel, out_shape=STRIPS + (f32(CAP, 2, PATCH, PATCH...  32.3 us
    pallas_call x1, Pallas kernels, run_slots(): pl.pallas_call(slots_kernel, out_shape=(f32(2, TILE, TILE),) + STRIPS + (...  15.5 us
    pallas_call x1, Pallas kernels, finish(): pl.pallas_call(functools.partial(finish_kernel, rate), out_shape=(f32(2,...  6.03 us

profile of v3, /device:TPU:6, one launch (start us, length us, event | category | flops | bytes accessed | tf_op | source)
XLA Modules:
  0.0 94.9 jit_solution(367686688052305407)
XLA Ops:
  1.3 32.3 %shard_map.77 = (f32[2,64,1024]{2,1,0:T(8,128)}, f32[2,64,1024]{2,1,0:T(8,128)}, f32[2,512,128]{2,1,0:T(8,128)}, f32[2,512,128]{2,1,0:T(8,128)}, f32[2,64,128]{2...) custom-call(s32[1,1,2,64]{3,2,1,0:T(2,128)} %bitcast.3, ...), custom_call_target="tpu_custom_call" | custom-call | tf_op jit(solution)/shard_map/pallas_call | solution.py:262
  33.5 15.5 %shard_map.78 = (f32[2,1024,1024]{2,1,0:T(8,128)}, f32[2,64,1024]{2,1,0:T(8,128)}, f32[2,64,1024]{2,1,0:T(8,128)}, f32[2,512,128]{2,1,0:T(8,128)}, f32[2,512,128...) custom-call(s32[1,1,2,64]{3,2,1,0:T(2,128)} %bitcast.4, ...), custom_call_target="tpu_custom_call" | custom-call | tf_op jit(solution)/shard_map/pallas_call | solution.py:451
  49.1 39.7 %shard_map.79 = (f32[2,64,1024]{2,1,0:T(8,128)}, f32[2,64,1024]{2,1,0:T(8,128)}, f32[2,512,128]{2,1,0:T(8,128)}, f32[2,512,128]{2,1,0:T(8,128)}, f32[2,64,128]{2...) custom-call(f32[256,128]{1,0:T(8,128)} %get-tuple-element.42.h, ...), custom_call_target="tpu_custom_call" | custom-call | tf_op jit(solution)/shard_map/pallas_call | solution.py:573
  88.8 6.0 %shard_map.80 = (f32[2,1024,1024]{2,1,0:T(8,128)}, f32[2,128,128]{2,1,0:T(8,128)}) custom-call(f32[2,1024,1024]{2,1,0:T(8,128)} %get-tuple-element.41.core, f32[2,128,128]{2,1,0:T(8,128)} %ill.5, f32[2,128,128]{2,1,0:T(8,128)} %bitcast.2, f32[2,64,1024]{2,1,0:T(8,128)} %get-tuple-element.52.refs_0_, ...), custom_call_target="tpu_custom_call", output_to_operand_aliasing={{0}: (0, {})} | custom-call | tf_op jit(solution)/shard_map/pallas_call | solution.py:638

commit v4 on v3

--- a/solution.py
+++ b/solution.py
@@ -17,7 +17,7 @@
 CAP = 64
 LANE_TILES = TILE // PATCH
 GROUP = 16
-GROUP_FAR = 4
+GROUP_FAR = 8
 CHUNKS = 4
 PACE = (0, 0, 1, 2, 4)
 RING = 8
@@ -301,17 +301,13 @@
         for p in range(2) for t in range(LANE_TILES)
     ]
 
+    for copy in body_copies:
+        copy.start()
+
     def listed(s, sizes):
-        good = inside(pos[0, 0, 0, s], pos[0, 0, 1, s])
-
-        @pl.when(good)
-        def _():
-            near[sizes[0]] = s
-
-        @pl.when(jnp.logical_not(good))
-        def _():
-            far[sizes[1]] = s
-        step = good.astype(jnp.int32)
+        near[sizes[0]] = s
+        far[sizes[1]] = s
+        step = inside(pos[0, 0, 0, s], pos[0, 0, 1, s]).astype(jnp.int32)
         return sizes[0] + step, sizes[1] + 1 - step
 
     n_near, n_far = lax.fori_loop(0, count, listed, (jnp.int32(0), jnp.int32(0)))
@@ -330,8 +326,6 @@
     def _(j):
         amp_copy(j).start()
 
-    for copy in body_copies:
-        copy.start()
     halo_copies = []
     for d in range(8):
         views = border_views(ob, halo[d], d)
@@ -597,17 +591,18 @@
     reads = [pltpu.make_async_copy(hbm, vmem, sem.at[n]) for n, (vmem, hbm) in enumerate(parts)]
     writes = [pltpu.make_async_copy(vmem, hbm, sem.at[n]) for n, (vmem, hbm) in enumerate(parts)]
     fetches = [pltpu.make_async_copy(strips[d], held[d], strip_sem.at[d]) for d in range(8)]
+    for d, (da, db) in enumerate(DIRS):
+        @pl.when(exists(-da, -db))
+        def _():
+            fetches[d].start()
     for copy in reads:
         copy.start()
-    for d, (da, db) in enumerate(DIRS):
-        @pl.when(exists(-da, -db))
-        def _():
-            fetches[d].start()
     probe[...] = ill[...] + rate * total[...]
-    for copy in reads:
-        copy.wait()
     half = TILE // 2
-    for d, (da, db) in enumerate(DIRS):
+
+    def add(d):
+        da, db = DIRS[d]
+
         @pl.when(exists(-da, -db))
         def _():
             fetches[d].wait()
@@ -627,8 +622,20 @@
                     side[p, 0:half - HALF, :] += first[HALF:half]
                     side[p, half - HALF:TILE - PATCH, :] += second[0:half - HALF]
                     bottom[p, :, cols] += second[half - HALF:half]
-    for copy in writes:
-        copy.start()
+
+    for n in (0, 1, 2):
+        reads[n].wait()
+    add(2)
+    writes[2].start()
+    reads[3].wait()
+    add(3)
+    writes[3].start()
+    for d in (0, 4, 5):
+        add(d)
+    writes[0].start()
+    for d in (1, 6, 7):
+        add(d)
+    writes[1].start()
     for copy in writes:
         copy.wait()
 

time: 95.1 us -> 94.6 us (level)
    pallas_call x1, Pallas kernels: 15.5 us -> 17 us  [run_slots(): pl.pallas_call(slots_kernel, out_shape=(f32(2, TILE, TILE),) + STRIPS + (...]
    pallas_call x1, Pallas kernels: 39.7 us -> 38.7 us  [return_edges(): pl.pallas_call(return_kernel, out_shape=STRIPS + (f32(2, rows, SMALL_ROWS...]
where the time goes in v4:
time: 94.6 us; the launch traced here: 95 us
  Pallas kernels  93.7 us (99%)
  between operations  1.3 us (1%)
    pallas_call x1, Pallas kernels, return_edges(): pl.pallas_call(return_kernel, out_shape=STRIPS + (f32(2, rows, SMALL_ROWS...  38.7 us
    pallas_call x1, Pallas kernels, run_early(): pl.pallas_call(early_kernel, out_shape=STRIPS + (f32(CAP, 2, PATCH, PATCH...  32.3 us
    pallas_call x1, Pallas kernels, run_slots(): pl.pallas_call(slots_kernel, out_shape=(f32(2, TILE, TILE),) + STRIPS + (...  17 us
    pallas_call x1, Pallas kernels, finish(): pl.pallas_call(functools.partial(finish_kernel, rate), out_shape=(f32(2,...  5.75 us

profile of v4, /device:TPU:6, one launch (start us, length us, event | category | flops | bytes accessed | tf_op | source)
XLA Modules:
  0.0 95.0 jit_solution(13486236781654659548)
XLA Ops:
  1.3 32.3 %shard_map.77 = (f32[2,64,1024]{2,1,0:T(8,128)}, f32[2,64,1024]{2,1,0:T(8,128)}, f32[2,512,128]{2,1,0:T(8,128)}, f32[2,512,128]{2,1,0:T(8,128)}, f32[2,64,128]{2...) custom-call(s32[1,1,2,64]{3,2,1,0:T(2,128)} %bitcast.3, ...), custom_call_target="tpu_custom_call" | custom-call | tf_op jit(solution)/shard_map/pallas_call | solution.py:262
  33.5 17.0 %shard_map.78 = (f32[2,1024,1024]{2,1,0:T(8,128)}, f32[2,64,1024]{2,1,0:T(8,128)}, f32[2,64,1024]{2,1,0:T(8,128)}, f32[2,512,128]{2,1,0:T(8,128)}, f32[2,512,128...) custom-call(s32[1,1,2,64]{3,2,1,0:T(2,128)} %bitcast.4, ...), custom_call_target="tpu_custom_call" | custom-call | tf_op jit(solution)/shard_map/pallas_call | solution.py:445
  50.6 38.7 %shard_map.79 = (f32[2,64,1024]{2,1,0:T(8,128)}, f32[2,64,1024]{2,1,0:T(8,128)}, f32[2,512,128]{2,1,0:T(8,128)}, f32[2,512,128]{2,1,0:T(8,128)}, f32[2,64,128]{2...) custom-call(f32[256,128]{1,0:T(8,128)} %get-tuple-element.42.h, ...), custom_call_target="tpu_custom_call" | custom-call | tf_op jit(solution)/shard_map/pallas_call | solution.py:567
  89.3 5.8 %shard_map.80 = (f32[2,1024,1024]{2,1,0:T(8,128)}, f32[2,128,128]{2,1,0:T(8,128)}) custom-call(f32[2,1024,1024]{2,1,0:T(8,128)} %get-tuple-element.41.core, f32[2,128,128]{2,1,0:T(8,128)} %ill.5, f32[2,128,128]{2,1,0:T(8,128)} %bitcast.2, f32[2,64,1024]{2,1,0:T(8,128)} %get-tuple-element.52.refs_0_, ...), custom_call_target="tpu_custom_call", output_to_operand_aliasing={{0}: (0, {})} | custom-call | tf_op jit(solution)/shard_map/pallas_call | solution.py:645

commit v5 on v4

--- a/solution.py
+++ b/solution.py
@@ -19,7 +19,7 @@
 GROUP = 16
 GROUP_FAR = 8
 CHUNKS = 4
-PACE = (0, 0, 1, 2, 4)
+PACE = (0, 1, 2, 3, 4)
 RING = 8
 step_object = 0.25
 DIRS = ((1, 0), (-1, 0), (0, 1), (0, -1), (1, 1), (1, -1), (-1, 1), (-1, -1))

time: 94.6 us -> 95 us (level); the launches traced: 95 us -> 93.1 us
  Pallas kernels: 93.7 us -> 91.8 us
    pallas_call x1, Pallas kernels: 38.7 us -> 31.9 us  [return_edges(): pl.pallas_call(return_kernel, out_shape=STRIPS + (f32(2, rows, SMALL_ROWS...]
    pallas_call x1, Pallas kernels: 17 us -> 21.9 us  [run_slots(): pl.pallas_call(slots_kernel, out_shape=(f32(2, TILE, TILE),) + STRIPS + (...]
where the time goes in v5:
time: 95 us; the launch traced here: 93.1 us
  Pallas kernels  91.8 us (97%)
  between operations  1.3 us (1%)
    pallas_call x1, Pallas kernels, run_early(): pl.pallas_call(early_kernel, out_shape=STRIPS + (f32(CAP, 2, PATCH, PATCH...  32.3 us
    pallas_call x1, Pallas kernels, return_edges(): pl.pallas_call(return_kernel, out_shape=STRIPS + (f32(2, rows, SMALL_ROWS...  31.9 us
    pallas_call x1, Pallas kernels, run_slots(): pl.pallas_call(slots_kernel, out_shape=(f32(2, TILE, TILE),) + STRIPS + (...  21.9 us
    pallas_call x1, Pallas kernels, finish(): pl.pallas_call(functools.partial(finish_kernel, rate), out_shape=(f32(2,...  5.75 us

profile of v5, /device:TPU:6, one launch (start us, length us, event | category | flops | bytes accessed | tf_op | source)
XLA Modules:
  0.0 93.1 jit_solution(16168439938732924713)
XLA Ops:
  1.3 32.3 %shard_map.77 = (f32[2,64,1024]{2,1,0:T(8,128)}, f32[2,64,1024]{2,1,0:T(8,128)}, f32[2,512,128]{2,1,0:T(8,128)}, f32[2,512,128]{2,1,0:T(8,128)}, f32[2,64,128]{2...) custom-call(s32[1,1,2,64]{3,2,1,0:T(2,128)} %bitcast.3, ...), custom_call_target="tpu_custom_call" | custom-call | tf_op jit(solution)/shard_map/pallas_call | solution.py:262
  33.5 21.9 %shard_map.78 = (f32[2,1024,1024]{2,1,0:T(8,128)}, f32[2,64,1024]{2,1,0:T(8,128)}, f32[2,64,1024]{2,1,0:T(8,128)}, f32[2,512,128]{2,1,0:T(8,128)}, f32[2,512,128...) custom-call(s32[1,1,2,64]{3,2,1,0:T(2,128)} %bitcast.4, ...), custom_call_target="tpu_custom_call" | custom-call | tf_op jit(solution)/shard_map/pallas_call | solution.py:445
  55.5 31.9 %shard_map.79 = (f32[2,64,1024]{2,1,0:T(8,128)}, f32[2,64,1024]{2,1,0:T(8,128)}, f32[2,512,128]{2,1,0:T(8,128)}, f32[2,512,128]{2,1,0:T(8,128)}, f32[2,64,128]{2...) custom-call(f32[256,128]{1,0:T(8,128)} %get-tuple-element.42.h, ...), custom_call_target="tpu_custom_call" | custom-call | tf_op jit(solution)/shard_map/pallas_call | solution.py:567
  87.4 5.8 %shard_map.80 = (f32[2,1024,1024]{2,1,0:T(8,128)}, f32[2,128,128]{2,1,0:T(8,128)}) custom-call(f32[2,1024,1024]{2,1,0:T(8,128)} %get-tuple-element.41.core, f32[2,128,128]{2,1,0:T(8,128)} %ill.5, f32[2,128,128]{2,1,0:T(8,128)} %bitcast.2, f32[2,64,1024]{2,1,0:T(8,128)} %get-tuple-element.52.refs_0_, ...), custom_call_target="tpu_custom_call", output_to_operand_aliasing={{0}: (0, {})} | custom-call | tf_op jit(solution)/shard_map/pallas_call | solution.py:645
